TPU v7x, 256 devices: a whole 4x4x8 slice. The times are simulated.
256 devices in a mesh: seq: 16 (over z, x_lo), wt: 16 (over x_hi, y, core).
Axes of the slice: x: 4 (x_hi: 2, x_lo: 2; x = x_hi * 2 + x_lo), y: 4, z: 8, core: 2. Of those that a mesh axis runs over, the one named last changes fastest.
Arguments:
- frames: bfloat16 [4096, 4096], P('seq'), may hold values from -40 to 40
- attn_norm_gain: float32 [4096], replicated, may hold values from 0.1 to 1.9
- qkv_weight: bfloat16 [3, 4096, 4096], P(None, 'seq', 'wt'), may hold values from -4 to 4
- attn_out_weight: bfloat16 [4096, 4096], P('seq', 'wt'), may hold values from -0.125 to 0.125
- conv_norm_gain: float32 [4096], replicated, may hold values from 0.1 to 1.9
- glu_weight: bfloat16 [2, 4096, 4096], P(None, 'seq', 'wt'), may hold values from -0.09375 to 0.09375
- depth_kernel: float32 [31, 4096], P(None, 'wt'), may hold values from -1 to 1
- norm_scale: float32 [4096], P('wt'), may hold values from 0.5 to 2
- norm_shift: float32 [4096], P('wt'), may hold values from -3 to 3
- conv_out_weight: bfloat16 [4096, 4096], P('seq', 'wt'), may hold values from -0.125 to 0.125
Outputs:
- encoded: bfloat16 [4096, 4096], P('seq', 'wt')
All inputs are finite; a program needn't handle non-finite values.
Results may differ from a plain program's by a relative error of at most 0.014.
Values may be sent and summed in bfloat16 or wider, within the bound.
No kernel may reach another device: no remote copies, remote signals or barrier semaphores. Data moves between devices by JAX's collectives and lax.ppermute only.
A program may use at most 64 MiB of HBM per device.

v0:
```python
import jax
import jax.numpy as jnp
from jax import lax
from jax.experimental import pallas as pl
from jax.experimental.pallas import tpu as pltpu
from jax.sharding import Mesh, PartitionSpec as P

HEAD_DIM = 128
BF16 = jnp.bfloat16
F32 = jnp.float32
SEQ = ("z", "xl")
WT = ("xh", "y", "c")
CHIPS = ("xh", "y")


def shift(value, axis, step):
    count = lax.axis_size(axis)
    return lax.ppermute(value, axis, [(i, (i + step) % count) for i in range(count)])


def smem():
    return pl.BlockSpec(memory_space=pltpu.SMEM)


def vmem():
    return pl.BlockSpec(memory_space=pltpu.VMEM)


def hbm():
    return pl.BlockSpec(memory_space=pltpu.HBM)


def run_kernel(body, where, arrays, outs, scratch, megabytes, flops, moved, exps=0, pinned=(), out_specs=None):
    return pl.pallas_call(
        body,
        out_shape=outs,
        in_specs=[smem()] + [vmem()] * len(arrays) + [hbm()] * len(pinned),
        out_specs=out_specs or jax.tree.map(lambda _: vmem(), outs),
        scratch_shapes=scratch,
        compiler_params=pltpu.CompilerParams(vmem_limit_bytes=megabytes << 20),
        cost_estimate=pl.CostEstimate(flops=flops, bytes_accessed=moved, transcendentals=exps),
    )(where, *arrays, *pinned)


def fetch(sources, places, sems):
    copies = [pltpu.make_async_copy(a, b, sems.at[n]) for n, (a, b) in enumerate(zip(sources, places))]
    for copy in copies:
        copy.start()
    return copies


def dot(a, b):
    return jnp.dot(a, b, preferred_element_type=F32)


def dot_t(a, b):
    return lax.dot_general(a, b, (((1,), (1,)), ((), ())), preferred_element_type=F32)


def norm_blocks_kernel(where, frames, gain, mine, other):
    rows, width = frames.shape
    blocks = mine.shape[0]
    block = mine.shape[2]
    z, xl, core = where[0], where[1], where[2]
    step_rows = 32

    def chunk(i, carry):
        r = pl.ds(pl.multiple_of(i * step_rows, step_rows), step_rows)
        wide = frames[r, :].astype(F32)
        mean = jnp.mean(wide, axis=-1, keepdims=True)
        centered = wide - mean
        scale = lax.rsqrt(jnp.mean(centered * centered, axis=-1, keepdims=True) + 1e-05)
        for out, first, parity in ((mine, 0, xl), (other, core * other.shape[0], 1 - xl)):
            for j in range(out.shape[0]):
                owner = lax.rem(z + first + j, blocks) * 2 + parity
                cols = pl.ds(pl.multiple_of(owner * block, block), block)
                part = (frames[r, cols].astype(F32) - mean) * scale * gain[:, cols]
                out[j, r, :] = part.astype(BF16)
        return carry

    lax.fori_loop(0, rows // step_rows, chunk, 0)


def project_kernel(where, mine, got, swapped, *refs):
    pieces, (kv_keep, q_keep, send, weights, sems) = refs[:-5], refs[-5:]
    xl, core = where[1], where[2]
    low = [jnp.where(core == 0, got[j], swapped[j]) for j in range(4)]
    high = [jnp.where(core == 0, swapped[j], got[j]) for j in range(4)]
    half = pieces[4].shape[1]
    places = [weights.at[:, j] for j in range(4)] + [weights.at[:, 4, :half], weights.at[:, 4, half:]] + [weights.at[:, j] for j in range(5, 8)]
    copies = {}
    for m in (1, 2, 0):
        copies[m] = fetch([piece.at[m] for piece in pieces], [place.at[m] for place in places], sems.at[m])
    for m, keep, at in ((1, kv_keep, 0), (2, kv_keep, 1), (0, q_keep, 0)):
        for copy in copies[m]:
            copy.wait()
        for r, a in enumerate((mine, low + high)):
            acc = None
            for j in range(8):
                term = dot(a[j], weights[m, j])
                acc = term if acc is None else acc + term
            even, odd = acc[:, :HEAD_DIM], acc[:, HEAD_DIM:]
            keep[at, r] = jnp.where(xl == 0, even, odd)
            send[m, r] = jnp.where(xl == 0, odd, even).astype(BF16)


def attend_kernel(where, q_keep, got, *refs):
    parts, (mine, send, scores, held, sems) = refs[:-5], refs[-5:]
    scale = HEAD_DIM ** (-0.5)
    step_rows = 128
    chunk = held.shape[2] * held.shape[3]
    count = len(parts)
    copies = fetch(parts, [held.at[j] for j in range(count)], sems)
    for copy in copies:
        copy.wait()

    def piece(j, side):
        return held[j, side].reshape(chunk, HEAD_DIM)

    for r, out in enumerate((mine, send)):
        for i in range(0, q_keep.shape[2], step_rows):
            query = (q_keep[0, r, i : i + step_rows] + got[0, 1 - r, i : i + step_rows].astype(F32)).astype(BF16)
            best = None
            for j in range(count):
                part = dot_t(query, piece(j, 0))
                scores[:, j * chunk : (j + 1) * chunk] = part
                top = jnp.max(part, axis=-1, keepdims=True)
                best = top if best is None else jnp.maximum(best, top)
            total = jnp.zeros((step_rows, 1), F32)
            acc = jnp.zeros((step_rows, HEAD_DIM), F32)
            for j in range(count):
                weights = jnp.exp((scores[:, j * chunk : (j + 1) * chunk] - best) * scale)
                total = total + jnp.sum(weights, axis=-1, keepdims=True)
                acc = acc + dot(weights.astype(BF16), piece(j, 1))
            out[i : i + step_rows, :] = (acc / total).astype(BF16)


def spread_out(inputs, pairs, places, mine, other, same):
    for (near, far), place in zip(pairs, places):
        a = dot_t(inputs, near).astype(BF16)
        b = dot_t(inputs, far).astype(BF16)
        mine[place] = jnp.where(same, a, b)
        other[place] = jnp.where(same, b, a)


def project_out_kernel(where, own, got, weight, far_weight, mine, other):
    xl = where[1]
    a, b = own[...], got[...]
    heads = jnp.concatenate([jnp.where(xl == 0, a, b), jnp.where(xl == 0, b, a)], axis=1)
    blocks, rows, block = mine.shape
    pairs = [(weight[j * block : (j + 1) * block], far_weight[j * block : (j + 1) * block]) for j in range(blocks)]
    spread_out(heads, pairs, range(blocks), mine, other, where[2] == xl)


def glu_kernel(where, mine, other, gain, *refs):
    pieces, (gated, normed, weights, sems) = refs[:-4], refs[-4:]
    blocks, rows, block = mine.shape
    copies = fetch([piece.at[:4] for piece in pieces], [weights.at[j] for j in range(blocks)], sems)
    z, xl = where[0], where[1]
    same = where[2] == xl
    step_rows = 32
    width = 2 * blocks * block

    def chunk(i, carry):
        r = pl.ds(pl.multiple_of(i * step_rows, step_rows), step_rows)
        parts = []
        for j in range(blocks):
            at = lax.rem(z + j, blocks)
            a, b = mine[at, r, :], other[at, r, :]
            parts += [jnp.where(same, a, b).astype(F32), jnp.where(same, b, a).astype(F32)]
        mean = jnp.sum(sum(parts), axis=-1, keepdims=True) / width
        square = sum((p - mean) * (p - mean) for p in parts)
        scale = lax.rsqrt(jnp.sum(square, axis=-1, keepdims=True) / width + 1e-05)
        for n, p in enumerate(parts):
            parity = xl if n % 2 == 0 else 1 - xl
            cols = pl.ds(pl.multiple_of((lax.rem(z + n // 2, blocks) * 2 + parity) * block, block), block)
            normed[n, r, :] = ((p - mean) * scale * gain[:, cols]).astype(BF16)
        return carry

    lax.fori_loop(0, rows // step_rows, chunk, 0)
    for copy in copies:
        copy.wait()
    sums = [None, None]
    for n in range(2 * blocks):
        j = n // 2
        for m in range(2):
            term = dot(normed[n], weights[j, 2 * m + n % 2])
            sums[m] = term if sums[m] is None else sums[m] + term
    gated[...] = (sums[0] * jax.nn.sigmoid(sums[1])).astype(BF16)


def conv_kernel(where, gated, before, after, taps, scale, offset, *refs):
    pieces, (mine, other, padded, activated, weights, sems) = refs[:-6], refs[-6:]
    copies = fetch([piece.at[4:] for piece in pieces], [weights.at[j] for j in range(len(pieces))], sems)
    rows = gated.shape[0]
    rim = before.shape[0]
    seq = where[0] * 2 + where[1]
    padded[:rim] = jnp.where(seq > 0, before[...].astype(F32), 0.0)
    padded[rim : rim + rows] = gated[...].astype(F32)
    padded[rim + rows :] = jnp.where(seq < where[3] - 1, after[...].astype(F32), 0.0)
    count = taps.shape[0]
    first = rim - (count - 1) // 2
    for i in range(0, rows, 32):
        acc = None
        for k in range(count):
            term = taps[k : k + 1, :] * padded[i + first + k : i + first + k + 32, :]
            acc = term if acc is None else acc + term
        v = acc * scale[...] + offset[...]
        activated[i : i + 32, :] = (v * jax.nn.sigmoid(v)).astype(BF16)
    for copy in copies:
        copy.wait()
    pairs = [(weights[j, 0], weights[j, 1]) for j in range(8)]
    places = [lax.rem(where[0] + j, 8) for j in range(8)]
    spread_out(activated[...], pairs, places, mine, other, where[2] == where[1])


def residual_kernel(where, parts, frames, mixed, copies, held, sem, sems):
    block = mixed.shape[1]
    cols = pl.ds(pl.multiple_of(where[4] * block, block), block)
    copy = pltpu.make_async_copy(frames.at[:, cols], held, sem)
    copy.start()
    total = parts[0].astype(F32)
    for j in range(1, parts.shape[0]):
        total = total + parts[j].astype(F32)
    copy.wait()
    result = (held[...].astype(F32) + total).astype(BF16)
    mixed[...] = result
    count = copies.shape[0]
    for out in fetch([mixed] * count, [copies.at[j] for j in range(count)], sems):
        out.wait()


def both_ways(right, left):
    return shift(right, "z", 1), shift(left, "z", -1)


def pair_sum(mine, other):
    got = shift(other, "c", 1)
    return (mine.astype(F32) + got.astype(F32)).astype(BF16)


def exchange(parts):
    return lax.all_to_all(parts, CHIPS, 0, 0, tiled=True)


def local(
    frames,
    attn_norm_gain,
    qkv_weight,
    attn_out_weight,
    conv_norm_gain,
    glu_weight,
    depth_kernel,
    norm_scale,
    norm_shift,
    conv_out_weight,
):
    rows, width = frames.shape
    block = qkv_weight.shape[2]
    blocks = width // block // 2
    z, xl, core = (lax.axis_index(a) for a in ("z", "xl", "c"))
    where = jnp.stack([z, xl, core, lax.axis_size(SEQ), lax.axis_index(WT)]).astype(jnp.int32)
    S = jax.ShapeDtypeStruct

    step = lax.optimization_barrier
    out_weight = lax.all_gather(attn_out_weight, "z", axis=0, tiled=True)
    late = jnp.concatenate([glu_weight, conv_out_weight[None]])
    late_far = shift(late, "xl", 1)

    half = block // 2
    r1, l1 = both_ways(qkv_weight, qkv_weight)
    mine, other = run_kernel(
        norm_blocks_kernel, where, [frames, attn_norm_gain.reshape(1, width)],
        [S((blocks, rows, block), BF16), S((blocks // 2, rows, block), BF16)], [], 16, 10 * rows * width, 4 * rows * width)
    got = shift(other, "xl", 1)
    r2, l2 = both_ways(r1, l1)
    r3, l3 = both_ways(r2, l2)
    far = both_ways(r3[:, :half], l3[:, half:])
    swapped, late_far = step((shift(got, "c", 1), late_far))
    late = jnp.stack([late, late_far], axis=1).reshape(6, block, block)
    kv_keep, q_keep, send = run_kernel(
        project_kernel, where, [mine, got, swapped],
        [S((2, 2, rows, HEAD_DIM), F32), S((1, 2, rows, HEAD_DIM), F32), S((3, 2, rows, HEAD_DIM), BF16)],
        [pltpu.VMEM((3, blocks, block, block), BF16), pltpu.SemaphoreType.DMA((3, 9))], 60,
        6 * rows * width * block, 6 * block * block * 8 + 4 * rows * width,
        pinned=[qkv_weight, l1, l2, l3, *far, r3, r2, r1])
    got, late = step((shift(send, "xl", 1), late))
    kv = (kv_keep + got[1:, ::-1].astype(F32)).astype(BF16)

    kv_r1, kv_l1 = both_ways(kv, kv)
    kv_r2, kv_l2 = both_ways(kv_r1, kv_l1)
    kv_r3, kv_l3 = both_ways(kv_r2, kv_l2)
    out_weight = [out_weight, shift(out_weight, "xl", 1)]
    kv_r3, kv_l3, late_left = step((kv_r3, kv_l3, late))
    late_l1 = shift(late_left, "z", -1)
    kv_r4, late_right = step((shift(kv_r3, "z", 1), late))
    late_r1 = shift(late_right, "z", 1)
    own, away = run_kernel(
        attend_kernel, where, [q_keep, got], [S((rows, HEAD_DIM), BF16)] * 2,
        [pltpu.VMEM((128, 16 * rows), F32), pltpu.VMEM((blocks, 2, 2, rows, HEAD_DIM), BF16), pltpu.SemaphoreType.DMA((blocks,))], 32,
        8 * rows * 16 * rows * HEAD_DIM, 4 << 20, 2 * rows * 16 * rows,
        pinned=[kv, kv_l1, kv_l2, kv_l3, kv_r4, kv_r3, kv_r2, kv_r1])
    back, late_l1 = step((shift(away, "xl", 1), late_l1))
    blocks_out = [S((blocks, rows, block), BF16)] * 2
    mine, other = run_kernel(
        project_out_kernel, where, [own, back] + out_weight, blocks_out, [], 16,
        2 * rows * block * width, 4 << 20)
    other, late_r1, late_l1 = step((other, late_r1, late_l1))
    late_r2, late_l2 = both_ways(late_r1, late_l1)
    late_r3, late_l3 = both_ways(late_r2, late_l2)
    mixed, copies = run_kernel(
        residual_kernel, where, [exchange(pair_sum(mine, other))],
        [S((rows, block), BF16), S((blocks, rows, block), BF16)],
        [pltpu.VMEM((rows, block), BF16), pltpu.SemaphoreType.DMA, pltpu.SemaphoreType.DMA((blocks,))], 16,
        10 * rows * block, 20 * rows * block, pinned=[frames], out_specs=[vmem(), hbm()])
    late_l4 = shift(late_l3, "z", -1)
    mine, late_l4, late_r3 = step((exchange(copies), late_l4, late_r3))
    other = shift(mine, "c", 1)
    late = [late, late_l1, late_l2, late_l3, late_l4, late_r3, late_r2, late_r1]
    gated = run_kernel(
        glu_kernel, where, [mine, other, conv_norm_gain.reshape(1, width)],
        S((rows, block), BF16),
        [pltpu.VMEM((2 * blocks, rows, block), BF16), pltpu.VMEM((blocks, 4, block, block), BF16), pltpu.SemaphoreType.DMA((blocks,))], 48,
        4 * rows * block * width, 6 << 20, pinned=late)
    rim = 16
    before = shift(gated[rows - rim :], SEQ, 1)
    after = shift(gated[:rim], SEQ, -1)
    mine, other = run_kernel(
        conv_kernel, where,
        [gated, before, after, depth_kernel, norm_scale.reshape(1, block), norm_shift.reshape(1, block)],
        blocks_out,
        [pltpu.VMEM((rows + 2 * rim, block), F32), pltpu.VMEM((rows, block), BF16),
         pltpu.VMEM((blocks, 2, block, block), BF16), pltpu.SemaphoreType.DMA((blocks,))], 16,
        2 * rows * block * width, 4 << 20, pinned=late)
    total = jnp.sum(exchange(pair_sum(mine, other)).astype(F32), axis=0)
    return (mixed.astype(F32) + total).astype(BF16)


def solution(mesh):
    split = Mesh(mesh.devices.reshape(8, 2, 2, 4, 2), ("z", "xl", "xh", "y", "c"))
    in_specs = (
        P(SEQ, None),
        P(),
        P(None, SEQ, WT),
        P(SEQ, WT),
        P(),
        P(None, SEQ, WT),
        P(None, WT),
        P(WT),
        P(WT),
        P(SEQ, WT),
    )
    return jax.shard_map(local, mesh=split, in_specs=in_specs, out_specs=P(SEQ, WT), check_vma=False)
```

profile of v0, /device:TPU:1, one launch (start us, length us, event | category | flops | bytes accessed | tf_op | source)
XLA Modules:
  0.0 234.5 jit_solution(8507798998880851819)
XLA Ops:
  6.5 6.4 %collective-permute-start.3 = (bf16[3,256,256]{2,1,0:T(8,128)(2,1)}, bf16[3,256,256]{2,1,0:T(8,128)(2,1)S(1)}, u32[]{:S(2)}, u32[]{:S(2)}) collective-permute-start(bf16[3,256,256]{2,1,0:T(8,128)(2,1)} %refs_0_.1), channel_id=1, source_target_pairs={{0,224},{32,0},{64,32},{96,64},{128,96},{160,128},{192,160},{224,1... | collective-permute-start | bytes 1179656 | tf_op jit(solution)/shard_map/ppermute | solution.py:18
  21.0 3.3 %collective-permute-start.4 = (bf16[3,256,256]{2,1,0:T(8,128)(2,1)S(1)}, bf16[3,256,256]{2,1,0:T(8,128)(2,1)S(1)}, u32[]{:S(2)}, u32[]{:S(2)}) collective-permute-start(bf16[3,256,256]{2,1,0:T(8,128)(2,1)S(1)} %collective-permute-done.3.refs_1_), channel_id=1, source_target_pairs={{0,224},{32,0},{64,32},{96,64},{128,96},{160,128},{192,160},{224,1... | collective-permute-start | bytes 1179656 | tf_op jit(solution)/shard_map/ppermute | solution.py:18
  24.4 6.8 %collective-permute-done.4.refs_2_ = bf16[3,256,256]{2,1,0:T(8,128)(2,1)S(1)} collective-permute-done((bf16[3,256,256]{2,1,0:T(8,128)(2,1)S(1)}, bf16[3,256,256]{2,1,0:T(8,128)(2,1)S(1)}, u32[]{:S(2)}, u32[]{:S(2)}) %collective-permute-start.4) | collective-permute-done | bytes 393248 | tf_op jit(solution)/shard_map/ppermute | solution.py:18
  31.2 3.4 %collective-permute-start.5 = (bf16[3,256,256]{2,1,0:T(8,128)(2,1)S(1)}, bf16[3,256,256]{2,1,0:T(8,128)(2,1)S(1)}, u32[]{:S(2)}, u32[]{:S(2)}) collective-permute-start(bf16[3,256,256]{2,1,0:T(8,128)(2,1)S(1)} %collective-permute-done.4.refs_2_), channel_id=1, source_target_pairs={{0,224},{32,0},{64,32},{96,64},{128,96},{160,128},{192,160},{224,1... | collective-permute-start | bytes 1179656 | tf_op jit(solution)/shard_map/ppermute | solution.py:18
  40.6 3.5 %collective-permute-start.10 = (bf16[3,128,256]{2,1,0:T(8,128)(2,1)S(1)}, bf16[3,128,256]{2,1,0:T(8,128)(2,1)S(1)}, u32[]{:S(2)}, u32[]{:S(2)}) collective-permute-start(bf16[3,128,256]{2,1,0:T(8,128)(2,1)S(1)} %slice.21), channel_id=1, source_target_pairs={{0,224},{32,0},{64,32},{96,64},{128,96},{160,128},{192,160},{224,1... | collective-permute-start | bytes 589832 | tf_op jit(solution)/shard_map/ppermute | solution.py:18
  44.2 4.2 %collective-permute-done.2 = bf16[3,256,256]{2,1,0:T(8,128)(2,1)S(1)} collective-permute-done((bf16[3,256,256]{2,1,0:T(8,128)(2,1)S(1)}, bf16[3,256,256]{2,1,0:T(8,128)(2,1)S(1)}, u32[]{:S(2)}, u32[]{:S(2)}) %collective-permute-start.2) | collective-permute-done | bytes 393248 | tf_op jit(solution)/shard_map/ppermute | solution.py:18
  50.6 6.1 %shard_map.101 = (f32[2,2,256,128]{3,2,1,0:T(8,128)}, f32[1,2,256,128]{3,2,1,0:T(8,128)}, bf16[3,2,256,128]{3,2,1,0:T(8,128)(2,1)}) custom-call(s32[5]{0:T(128)} %copy-done.7, bf16[8,256,256]{2,1,0:T(8,128)(2,1)} %copy-done.13, bf16[4,256,256]{2,1,0:T(8,128)(2,1)} %copy-done.21, bf16[4,256,256]{2,1,0:T(8,128)(2,1)} %copy-done.22, ...), custom_call_target="tpu_custom_call" | custom-call | flops 1610612736 | bytes 7340032 | tf_op jit(solution)/shard_map/pallas_call | solution.py:34
  58.1 5.9 %collective-permute-done.11.got = bf16[3,2,256,128]{3,2,1,0:T(8,128)(2,1)S(1)} collective-permute-done((bf16[3,2,256,128]{3,2,1,0:T(8,128)(2,1)}, bf16[3,2,256,128]{3,2,1,0:T(8,128)(2,1)S(1)}, u32[]{:S(2)}, u32[]{:S(2)}) %collective-permute-start.11) | collective-permute-done | bytes 393248 | tf_op jit(solution)/shard_map/ppermute | solution.py:18
  66.8 6.0 %collective-permute-done.14.refs_7_ = bf16[2,2,256,128]{3,2,1,0:T(8,128)(2,1)S(1)} collective-permute-done((bf16[2,2,256,128]{3,2,1,0:T(8,128)(2,1)S(1)}, bf16[2,2,256,128]{3,2,1,0:T(8,128)(2,1)S(1)}, u32[]{:S(2)}, u32[]{:S(2)}) %collective-permute-start.14) | collective-permute-done | bytes 262176 | tf_op jit(solution)/shard_map/ppermute | solution.py:18
  75.6 5.9 %collective-permute-done.15.refs_6_ = bf16[2,2,256,128]{3,2,1,0:T(8,128)(2,1)S(1)} collective-permute-done((bf16[2,2,256,128]{3,2,1,0:T(8,128)(2,1)S(1)}, bf16[2,2,256,128]{3,2,1,0:T(8,128)(2,1)S(1)}, u32[]{:S(2)}, u32[]{:S(2)}) %collective-permute-start.15) | collective-permute-done | bytes 262176 | tf_op jit(solution)/shard_map/ppermute | solution.py:18
  85.6 5.0 %collective-permute-done.16.refs_5_ = bf16[2,2,256,128]{3,2,1,0:T(8,128)(2,1)S(1)} collective-permute-done((bf16[2,2,256,128]{3,2,1,0:T(8,128)(2,1)S(1)}, bf16[2,2,256,128]{3,2,1,0:T(8,128)(2,1)S(1)}, u32[]{:S(2)}, u32[]{:S(2)}) %collective-permute-start.16) | collective-permute-done | bytes 262176 | tf_op jit(solution)/shard_map/ppermute | solution.py:18
  93.2 5.5 %collective-permute-done.18.refs_4_ = bf16[2,2,256,128]{3,2,1,0:T(8,128)(2,1)S(1)} collective-permute-done((bf16[2,2,256,128]{3,2,1,0:T(8,128)(2,1)S(1)}, bf16[2,2,256,128]{3,2,1,0:T(8,128)(2,1)S(1)}, u32[]{:S(2)}, u32[]{:S(2)}) %collective-permute-start.18) | collective-permute-done | bytes 262176 | tf_op jit(solution)/shard_map/ppermute | solution.py:18
  98.8 4.9 %shard_map.102 = (bf16[256,128]{1,0:T(8,128)(2,1)S(1)}, bf16[256,128]{1,0:T(8,128)(2,1)S(1)}) custom-call(s32[5]{0:T(128)S(1)} %copy-done.8, f32[1,2,256,128]{3,2,1,0:T(8,128)S(1)} %copy-done.14, bf16[3,2,256,128]{3,2,1,0:T(8,128)(2,1)S(1)} %collective-permute-done.11.got, bf16[2,2,256,128]{3,2,1,0:T(8,128)(2,1)S(1)} %add_convert_fusion.2.refs_0_, ...), custom_call_target="tpu_custom_call" | custom-call | flops 1073741824 | bytes 4194304 | tf_op jit(solution)/shard_map/pallas_call | solution.py:34
  104.8 3.3 %collective-permute-done.19.got = bf16[256,128]{1,0:T(8,128)(2,1)S(1)} collective-permute-done((bf16[256,128]{1,0:T(8,128)(2,1)S(1)}, bf16[256,128]{1,0:T(8,128)(2,1)S(1)}, u32[]{:S(2)}, u32[]{:S(2)}) %collective-permute-start.19) | collective-permute-done | bytes 65568 | tf_op jit(solution)/shard_map/ppermute | solution.py:18
  109.4 4.2 %collective-permute-done.22.refs_7_ = bf16[6,256,256]{2,1,0:T(8,128)(2,1)S(1)} collective-permute-done((bf16[6,256,256]{2,1,0:T(8,128)(2,1)S(1)}, bf16[6,256,256]{2,1,0:T(8,128)(2,1)S(1)}, u32[]{:S(2)}, u32[]{:S(2)}) %collective-permute-start.22) | collective-permute-done | bytes 786464 | tf_op jit(solution)/shard_map/ppermute | solution.py:18
  113.6 11.9 %collective-permute-start.23 = (bf16[8,256,256]{2,1,0:T(8,128)(2,1)S(1)}, bf16[8,256,256]{2,1,0:T(8,128)(2,1)S(1)}, u32[]{:S(2)}, u32[]{:S(2)}) collective-permute-start(bf16[8,256,256]{2,1,0:T(8,128)(2,1)S(1)} %get-tuple-element.55), channel_id=1, source_target_pairs={{0,1},{1,0},{2,3},{3,2},{4,5},{5,4},{6,7},{7,6},{8,9},{9,8},{10,11... | collective-permute-start | bytes 3145736 | tf_op jit(solution)/shard_map/ppermute | solution.py:18
  129.1 7.1 %all-to-all-start = ((bf16[8,256,256]{2,1,0:T(8,128)(2,1)}), bf16[8,256,256]{2,1,0:T(8,128)(2,1)}, u32[]{:S(2)}, u32[]{:S(2)}) async-start(bf16[8,256,256]{2,1,0:T(8,128)(2,1)} %add_convert_fusion.1), calls=%async_computation | async-start | bytes 2097152 | tf_op jit(solution)/shard_map/all_to_all | solution.py:243
  136.2 8.8 %collective-permute-done.24.refs_2_ = bf16[6,256,256]{2,1,0:T(8,128)(2,1)} collective-permute-done((bf16[6,256,256]{2,1,0:T(8,128)(2,1)}, bf16[6,256,256]{2,1,0:T(8,128)(2,1)}, u32[]{:S(2)}, u32[]{:S(2)}) %collective-permute-start.24) | collective-permute-done | bytes 786464 | tf_op jit(solution)/shard_map/ppermute | solution.py:18
  146.3 4.4 %all-to-all-done.parts = bf16[8,256,256]{2,1,0:T(8,128)(2,1)} async-done(((bf16[8,256,256]{2,1,0:T(8,128)(2,1)}), bf16[8,256,256]{2,1,0:T(8,128)(2,1)}, u32[]{:S(2)}, u32[]{:S(2)}) %all-to-all-start) | async-done | bytes 1048608 | tf_op jit(solution)/shard_map/all_to_all | solution.py:243
  154.6 5.6 %all-to-all-start.1 = ((bf16[8,256,256]{2,1,0:T(8,128)(2,1)}), bf16[8,256,256]{2,1,0:T(8,128)(2,1)}, u32[]{:S(2)}, u32[]{:S(2)}) async-start(bf16[8,256,256]{2,1,0:T(8,128)(2,1)} %copy-done.5), calls=%async_computation.1 | async-start | bytes 2097152 | tf_op jit(solution)/shard_map/all_to_all | solution.py:243
  160.3 3.3 %collective-permute-done.25.refs_3_ = bf16[6,256,256]{2,1,0:T(8,128)(2,1)} collective-permute-done((bf16[6,256,256]{2,1,0:T(8,128)(2,1)}, bf16[6,256,256]{2,1,0:T(8,128)(2,1)}, u32[]{:S(2)}, u32[]{:S(2)}) %collective-permute-start.25) | collective-permute-done | bytes 786464 | tf_op jit(solution)/shard_map/ppermute | solution.py:18
  165.7 14.3 %collective-permute-done.28.refs_5_ = bf16[6,256,256]{2,1,0:T(8,128)(2,1)S(1)} collective-permute-done((bf16[6,256,256]{2,1,0:T(8,128)(2,1)}, bf16[6,256,256]{2,1,0:T(8,128)(2,1)S(1)}, u32[]{:S(2)}, u32[]{:S(2)}) %collective-permute-start.28) | collective-permute-done | bytes 786464 | tf_op jit(solution)/shard_map/ppermute | solution.py:18
  187.3 5.4 %shard_map.105.gated = bf16[256,256]{1,0:T(8,128)(2,1)S(1)} custom-call(s32[5]{0:T(128)S(1)} %copy-done.8, bf16[8,256,256]{2,1,0:T(8,128)(2,1)} %all-to-all-done.1.mine, bf16[8,256,256]{2,1,0:T(8,128)(2,1)} %copy-done.15, f32[1,4096]{1,0:T(1,128)S(1)} %bitcast.18, bf16[6,256,256]{2,1,0:T(8,128)(2,1)S(1)} %bitcast.15, ...), custom_call_target="tpu_custom_call" | custom-call | flops 1073741824 | bytes 6291456 | tf_op jit(solution)/shard_map/pallas_call | solution.py:34
  204.8 22.1 %all_to_all.15 = bf16[8,256,256]{2,1,0:T(8,128)(2,1)S(1)} all-to-all(bf16[8,256,256]{2,1,0:T(8,128)(2,1)S(1)} %add_convert_fusion), channel_id=1, replica_groups=mesh['z'=8,'xl'=2,'xh'=2,'y'=4,'c'=2] {'xh','y'}, dimensions={0} | all-to-all | bytes 2097152 | tf_op jit(solution)/shard_map/all_to_all | solution.py:243
  (126 shorter events, 63.6 us)
Async XLA Ops:
  6.5 77.7 %all-gather.2.cloned.1.call-start = ((), (), s32[]{:S(2)}) async-start(), calls=%async_computation.3 | async-start | bytes 1179648 | tf_op jit(solution)/shard_map/all_gather | solution.py:266
  6.5 14.5 %collective-permute-start.3 = (bf16[3,256,256]{2,1,0:T(8,128)(2,1)}, bf16[3,256,256]{2,1,0:T(8,128)(2,1)S(1)}, u32[]{:S(2)}, u32[]{:S(2)}) collective-permute-start(bf16[3,256,256]{2,1,0:T(8,128)(2,1)} %refs_0_.1), channel_id=1, source_target_pairs={{0,224},{32,0},{64,32},{96,64},{128,96},{160,128},{192,160},{224,1... | collective-permute-start | bytes 1179656 | tf_op jit(solution)/shard_map/ppermute | solution.py:18
  12.9 11.4 %collective-permute-start.6 = (bf16[3,256,256]{2,1,0:T(8,128)(2,1)}, bf16[3,256,256]{2,1,0:T(8,128)(2,1)S(1)}, u32[]{:S(2)}, u32[]{:S(2)}) collective-permute-start(bf16[3,256,256]{2,1,0:T(8,128)(2,1)} %refs_0_.1), channel_id=1, source_target_pairs={{0,32},{32,64},{64,96},{96,128},{128,160},{160,192},{192,224},{224... | collective-permute-start | bytes 1179656 | tf_op jit(solution)/shard_map/ppermute | solution.py:18
  19.2 15.4 %collective-permute-start = (bf16[4,256,256]{2,1,0:T(8,128)(2,1)S(1)}, bf16[4,256,256]{2,1,0:T(8,128)(2,1)S(1)}, u32[]{:S(2)}, u32[]{:S(2)}) collective-permute-start(bf16[4,256,256]{2,1,0:T(8,128)(2,1)S(1)} %get-tuple-element.36), channel_id=1, source_target_pairs={{0,16},{16,0},{1,17},{17,1},{2,18},{18,2},{3,19},{19,3},{4,20},{20... | collective-permute-start | bytes 1572872 | tf_op jit(solution)/shard_map/ppermute | solution.py:18
  21.0 10.2 %collective-permute-start.4 = (bf16[3,256,256]{2,1,0:T(8,128)(2,1)S(1)}, bf16[3,256,256]{2,1,0:T(8,128)(2,1)S(1)}, u32[]{:S(2)}, u32[]{:S(2)}) collective-permute-start(bf16[3,256,256]{2,1,0:T(8,128)(2,1)S(1)} %collective-permute-done.3.refs_1_), channel_id=1, source_target_pairs={{0,224},{32,0},{64,32},{96,64},{128,96},{160,128},{192,160},{224,1... | collective-permute-start | bytes 1179656 | tf_op jit(solution)/shard_map/ppermute | solution.py:18
  24.4 10.3 %collective-permute-start.7 = (bf16[3,256,256]{2,1,0:T(8,128)(2,1)S(1)}, bf16[3,256,256]{2,1,0:T(8,128)(2,1)}, u32[]{:S(2)}, u32[]{:S(2)}) collective-permute-start(bf16[3,256,256]{2,1,0:T(8,128)(2,1)S(1)} %collective-permute-done.6.refs_8_), channel_id=1, source_target_pairs={{0,32},{32,64},{64,96},{96,128},{128,160},{160,192},{192,224},{224... | collective-permute-start | bytes 1179656 | tf_op jit(solution)/shard_map/ppermute | solution.py:18
  31.2 9.4 %collective-permute-start.5 = (bf16[3,256,256]{2,1,0:T(8,128)(2,1)S(1)}, bf16[3,256,256]{2,1,0:T(8,128)(2,1)S(1)}, u32[]{:S(2)}, u32[]{:S(2)}) collective-permute-start(bf16[3,256,256]{2,1,0:T(8,128)(2,1)S(1)} %collective-permute-done.4.refs_2_), channel_id=1, source_target_pairs={{0,224},{32,0},{64,32},{96,64},{128,96},{160,128},{192,160},{224,1... | collective-permute-start | bytes 1179656 | tf_op jit(solution)/shard_map/ppermute | solution.py:18
  34.6 9.4 %collective-permute-start.8 = (bf16[3,256,256]{2,1,0:T(8,128)(2,1)}, bf16[3,256,256]{2,1,0:T(8,128)(2,1)S(1)}, u32[]{:S(2)}, u32[]{:S(2)}) collective-permute-start(bf16[3,256,256]{2,1,0:T(8,128)(2,1)} %collective-permute-done.7.refs_7_), channel_id=1, source_target_pairs={{0,32},{32,64},{64,96},{96,128},{128,160},{160,192},{192,224},{224... | collective-permute-start | bytes 1179656 | tf_op jit(solution)/shard_map/ppermute | solution.py:18
  34.7 13.7 %collective-permute-start.1 = (bf16[4,256,256]{2,1,0:T(8,128)(2,1)S(1)}, bf16[4,256,256]{2,1,0:T(8,128)(2,1)S(1)}, u32[]{:S(2)}, u32[]{:S(2)}) collective-permute-start(bf16[4,256,256]{2,1,0:T(8,128)(2,1)S(1)} %collective-permute-done.got), channel_id=1, source_target_pairs={{0,1},{1,0},{2,3},{3,2},{4,5},{5,4},{6,7},{7,6},{8,9},{9,8},{10,11... | collective-permute-start | bytes 1572872 | tf_op jit(solution)/shard_map/ppermute | solution.py:18
  37.6 10.8 %collective-permute-start.2 = (bf16[3,256,256]{2,1,0:T(8,128)(2,1)S(1)}, bf16[3,256,256]{2,1,0:T(8,128)(2,1)S(1)}, u32[]{:S(2)}, u32[]{:S(2)}) collective-permute-start(bf16[3,256,256]{2,1,0:T(8,128)(2,1)S(1)} %get-tuple-element.66), channel_id=1, source_target_pairs={{0,16},{16,0},{1,17},{17,1},{2,18},{18,2},{3,19},{19,3},{4,20},{20... | collective-permute-start | bytes 1179656 | tf_op jit(solution)/shard_map/ppermute | solution.py:18
  64.1 8.8 %collective-permute-start.14 = (bf16[2,2,256,128]{3,2,1,0:T(8,128)(2,1)S(1)}, bf16[2,2,256,128]{3,2,1,0:T(8,128)(2,1)S(1)}, u32[]{:S(2)}, u32[]{:S(2)}) collective-permute-start(bf16[2,2,256,128]{3,2,1,0:T(8,128)(2,1)S(1)} %add_convert_fusion.2.refs_0_), channel_id=1, source_target_pairs={{0,32},{32,64},{64,96},{96,128},{128,160},{160,192},{192,224},{224... | collective-permute-start | bytes 786440 | tf_op jit(solution)/shard_map/ppermute | solution.py:18
  81.5 9.1 %collective-permute-start.16 = (bf16[2,2,256,128]{3,2,1,0:T(8,128)(2,1)S(1)}, bf16[2,2,256,128]{3,2,1,0:T(8,128)(2,1)S(1)}, u32[]{:S(2)}, u32[]{:S(2)}) collective-permute-start(bf16[2,2,256,128]{3,2,1,0:T(8,128)(2,1)S(1)} %collective-permute-done.15.refs_6_), channel_id=1, source_target_pairs={{0,32},{32,64},{64,96},{96,128},{128,160},{160,192},{192,224},{224... | collective-permute-start | bytes 786440 | tf_op jit(solution)/shard_map/ppermute | solution.py:18
  81.5 9.1 %collective-permute-start.17 = (bf16[2,2,256,128]{3,2,1,0:T(8,128)(2,1)S(1)}, bf16[2,2,256,128]{3,2,1,0:T(8,128)(2,1)S(1)}, u32[]{:S(2)}, u32[]{:S(2)}) collective-permute-start(bf16[2,2,256,128]{3,2,1,0:T(8,128)(2,1)S(1)} %collective-permute-done.13.refs_2_), channel_id=1, source_target_pairs={{0,224},{32,0},{64,32},{96,64},{128,96},{160,128},{192,160},{224,1... | collective-permute-start | bytes 786440 | tf_op jit(solution)/shard_map/ppermute | solution.py:18
  84.2 23.9 %collective-permute-start.21 = (bf16[2048,256]{1,0:T(8,128)(2,1)}, bf16[2048,256]{1,0:T(8,128)(2,1)S(1)}, u32[]{:S(2)}, u32[]{:S(2)}) collective-permute-start(bf16[2048,256]{1,0:T(8,128)(2,1)} %all-gather.2.cloned.1.call-done.weight), channel_id=1, source_target_pairs={{0,16},{16,0},{1,17},{17,1},{2,18},{18,2},{3,19},{19,3},{4,20},{20... | collective-permute-start | bytes 3145736 | tf_op jit(solution)/shard_map/ppermute | solution.py:18
  90.6 17.5 %collective-permute-start.20 = (bf16[6,256,256]{2,1,0:T(8,128)(2,1)S(1)}, bf16[6,256,256]{2,1,0:T(8,128)(2,1)}, u32[]{:S(2)}, u32[]{:S(2)}) collective-permute-start(bf16[6,256,256]{2,1,0:T(8,128)(2,1)S(1)} %bitcast.13), channel_id=1, source_target_pairs={{0,224},{32,0},{64,32},{96,64},{128,96},{160,128},{192,160},{224,1... | collective-permute-start | bytes 2359304 | tf_op jit(solution)/shard_map/ppermute | solution.py:18
  98.8 14.9 %collective-permute-start.22 = (bf16[6,256,256]{2,1,0:T(8,128)(2,1)S(1)}, bf16[6,256,256]{2,1,0:T(8,128)(2,1)S(1)}, u32[]{:S(2)}, u32[]{:S(2)}) collective-permute-start(bf16[6,256,256]{2,1,0:T(8,128)(2,1)S(1)} %bitcast.14), channel_id=1, source_target_pairs={{0,32},{32,64},{64,96},{96,128},{128,160},{160,192},{192,224},{224... | collective-permute-start | bytes 2359304 | tf_op jit(solution)/shard_map/ppermute | solution.py:18
  113.6 14.2 %collective-permute-start.23 = (bf16[8,256,256]{2,1,0:T(8,128)(2,1)S(1)}, bf16[8,256,256]{2,1,0:T(8,128)(2,1)S(1)}, u32[]{:S(2)}, u32[]{:S(2)}) collective-permute-start(bf16[8,256,256]{2,1,0:T(8,128)(2,1)S(1)} %get-tuple-element.55), channel_id=1, source_target_pairs={{0,1},{1,0},{2,3},{3,2},{4,5},{5,4},{6,7},{7,6},{8,9},{9,8},{10,11... | collective-permute-start | bytes 3145736 | tf_op jit(solution)/shard_map/ppermute | solution.py:18
  125.5 19.5 %collective-permute-start.24 = (bf16[6,256,256]{2,1,0:T(8,128)(2,1)}, bf16[6,256,256]{2,1,0:T(8,128)(2,1)}, u32[]{:S(2)}, u32[]{:S(2)}) collective-permute-start(bf16[6,256,256]{2,1,0:T(8,128)(2,1)} %collective-permute-done.20.refs_1_), channel_id=1, source_target_pairs={{0,224},{32,0},{64,32},{96,64},{128,96},{160,128},{192,160},{224,1... | collective-permute-start | bytes 2359304 | tf_op jit(solution)/shard_map/ppermute | solution.py:18
  129.1 21.7 %all-to-all-start = ((bf16[8,256,256]{2,1,0:T(8,128)(2,1)}), bf16[8,256,256]{2,1,0:T(8,128)(2,1)}, u32[]{:S(2)}, u32[]{:S(2)}) async-start(bf16[8,256,256]{2,1,0:T(8,128)(2,1)} %add_convert_fusion.1), calls=%async_computation | async-start | bytes 2097152 | tf_op jit(solution)/shard_map/all_to_all | solution.py:243
  136.1 24.1 %collective-permute-start.27 = (bf16[6,256,256]{2,1,0:T(8,128)(2,1)}, bf16[6,256,256]{2,1,0:T(8,128)(2,1)}, u32[]{:S(2)}, u32[]{:S(2)}) collective-permute-start(bf16[6,256,256]{2,1,0:T(8,128)(2,1)} %copy-done.2), channel_id=1, source_target_pairs={{0,32},{32,64},{64,96},{96,128},{128,160},{160,192},{192,224},{224... | collective-permute-start | bytes 2359304 | tf_op jit(solution)/shard_map/ppermute | solution.py:18
  145.0 18.6 %collective-permute-start.25 = (bf16[6,256,256]{2,1,0:T(8,128)(2,1)}, bf16[6,256,256]{2,1,0:T(8,128)(2,1)}, u32[]{:S(2)}, u32[]{:S(2)}) collective-permute-start(bf16[6,256,256]{2,1,0:T(8,128)(2,1)} %collective-permute-done.24.refs_2_), channel_id=1, source_target_pairs={{0,224},{32,0},{64,32},{96,64},{128,96},{160,128},{192,160},{224,1... | collective-permute-start | bytes 2359304 | tf_op jit(solution)/shard_map/ppermute | solution.py:18
  154.6 26.5 %all-to-all-start.1 = ((bf16[8,256,256]{2,1,0:T(8,128)(2,1)}), bf16[8,256,256]{2,1,0:T(8,128)(2,1)}, u32[]{:S(2)}, u32[]{:S(2)}) async-start(bf16[8,256,256]{2,1,0:T(8,128)(2,1)} %copy-done.5), calls=%async_computation.1 | async-start | bytes 2097152 | tf_op jit(solution)/shard_map/all_to_all | solution.py:243
  160.2 19.8 %collective-permute-start.28 = (bf16[6,256,256]{2,1,0:T(8,128)(2,1)}, bf16[6,256,256]{2,1,0:T(8,128)(2,1)S(1)}, u32[]{:S(2)}, u32[]{:S(2)}) collective-permute-start(bf16[6,256,256]{2,1,0:T(8,128)(2,1)} %collective-permute-done.27.refs_6_), channel_id=1, source_target_pairs={{0,32},{32,64},{64,96},{96,128},{128,160},{160,192},{192,224},{224... | collective-permute-start | bytes 2359304 | tf_op jit(solution)/shard_map/ppermute | solution.py:18
  163.6 17.6 %collective-permute-start.26 = (bf16[6,256,256]{2,1,0:T(8,128)(2,1)}, bf16[6,256,256]{2,1,0:T(8,128)(2,1)S(1)}, u32[]{:S(2)}, u32[]{:S(2)}) collective-permute-start(bf16[6,256,256]{2,1,0:T(8,128)(2,1)} %collective-permute-done.25.refs_3_), channel_id=1, source_target_pairs={{0,224},{32,0},{64,32},{96,64},{128,96},{160,128},{192,160},{224,1... | collective-permute-start | bytes 2359304 | tf_op jit(solution)/shard_map/ppermute | solution.py:18
  (40 other events, 471.7 us)
Sparse Core Ops, SparseCore 0:
  39.0 33.1 all-gather.1
where the time goes:
time: 235 us
  waiting for transfers between devices  90.2 us (38%)
  starting transfers between devices  73.8 us (31%)
  Pallas kernels  26.1 us (11%)
  blocking collectives  22.1 us (9%)
  between operations  13.7 us (6%)
  local copies, waits for them, and re-layouts  6.15 us (3%)
  other arithmetic  2.51 us (1%)
    ppermute x33, waiting for transfers between devices, shift(): lax.ppermute(value, axis, [(i, (i + step) % count) for i in range(count)])  85.8 us
    ppermute x33, starting transfers between devices, shift(): lax.ppermute(value, axis, [(i, (i + step) % count) for i in range(count)])  61.1 us
    pallas_call x7, Pallas kernels, run_kernel(): pl.pallas_call(body, out_shape=outs, in_specs=[smem()] + [vmem()] * len(a...  26.1 us
    all_to_all x1, blocking collectives, exchange(): return lax.all_to_all(parts, CHIPS, 0, 0, tiled=True)  22.1 us
    all_to_all x2, starting transfers between devices, exchange(): return lax.all_to_all(parts, CHIPS, 0, 0, tiled=True)  12.7 us
    unnamed x56, local copies, waits for them, and re-layouts  5.96 us
  transfers between devices with their start and end apart: 36, of which 21 were waited for; matrix products, arithmetic and copies ran while one was open for 1% of the time, Pallas kernels for 8%

commit v1 on v0

--- a/solution.py
+++ b/solution.py
@@ -81,58 +81,103 @@
     lax.fori_loop(0, rows // step_rows, chunk, 0)
 
 
-def project_kernel(where, mine, got, swapped, *refs):
+def both_rows(mine, got, swapped, core):
+    low = [jnp.where(core == 0, got[j], swapped[j]) for j in range(4)]
+    high = [jnp.where(core == 0, swapped[j], got[j]) for j in range(4)]
+    return mine, low + high
+
+
+EARLY = (0, 1, 2, 6, 7)
+LATE = (3, 4, 5)
+
+
+def project_early_kernel(where, mine, got, swapped, *refs):
+    pieces, (sums, weights, sems) = refs[:-3], refs[-3:]
+    copies = fetch(pieces, [weights.at[n] for n in range(len(pieces))], sems)
+    sides = both_rows(mine, got, swapped, where[2])
+    for copy in copies:
+        copy.wait()
+    for m in range(3):
+        for r, a in enumerate(sides):
+            acc = None
+            for n, j in enumerate(EARLY):
+                term = dot(a[j], weights[n, m])
+                acc = term if acc is None else acc + term
+            sums[m, r] = acc
+
+
+def project_kernel(where, mine, got, swapped, sums, *refs):
     pieces, (kv_keep, q_keep, send, weights, sems) = refs[:-5], refs[-5:]
     xl, core = where[1], where[2]
-    low = [jnp.where(core == 0, got[j], swapped[j]) for j in range(4)]
-    high = [jnp.where(core == 0, swapped[j], got[j]) for j in range(4)]
-    half = pieces[4].shape[1]
-    places = [weights.at[:, j] for j in range(4)] + [weights.at[:, 4, :half], weights.at[:, 4, half:]] + [weights.at[:, j] for j in range(5, 8)]
-    copies = {}
-    for m in (1, 2, 0):
-        copies[m] = fetch([piece.at[m] for piece in pieces], [place.at[m] for place in places], sems.at[m])
+    half = pieces[1].shape[1]
+    copies = fetch(pieces, [weights.at[0], weights.at[1, :, :half], weights.at[1, :, half:], weights.at[2]], sems)
+    sides = both_rows(mine, got, swapped, core)
+    for copy in copies:
+        copy.wait()
     for m, keep, at in ((1, kv_keep, 0), (2, kv_keep, 1), (0, q_keep, 0)):
-        for copy in copies[m]:
-            copy.wait()
-        for r, a in enumerate((mine, low + high)):
-            acc = None
-            for j in range(8):
-                term = dot(a[j], weights[m, j])
-                acc = term if acc is None else acc + term
+        for r, a in enumerate(sides):
+            acc = sums[m, r]
+            for n, j in enumerate(LATE):
+                acc = acc + dot(a[j], weights[n, m])
             even, odd = acc[:, :HEAD_DIM], acc[:, HEAD_DIM:]
             keep[at, r] = jnp.where(xl == 0, even, odd)
             send[m, r] = jnp.where(xl == 0, odd, even).astype(BF16)
 
 
-def attend_kernel(where, q_keep, got, *refs):
-    parts, (mine, send, scores, held, sems) = refs[:-5], refs[-5:]
+def attend_rows(query, held, scores):
     scale = HEAD_DIM ** (-0.5)
-    step_rows = 128
+    count = held.shape[0]
     chunk = held.shape[2] * held.shape[3]
-    count = len(parts)
-    copies = fetch(parts, [held.at[j] for j in range(count)], sems)
+    best = None
+    for j in range(count):
+        part = dot_t(query, held[j, 0].reshape(chunk, HEAD_DIM))
+        scores[:, j * chunk : (j + 1) * chunk] = part
+        top = jnp.max(part, axis=-1, keepdims=True)
+        best = top if best is None else jnp.maximum(best, top)
+    total, acc = None, None
+    for j in range(count):
+        weights = jnp.exp((scores[:, j * chunk : (j + 1) * chunk] - best) * scale)
+        row_sum = jnp.sum(weights, axis=-1, keepdims=True)
+        term = dot(weights.astype(BF16), held[j, 1].reshape(chunk, HEAD_DIM))
+        total = row_sum if total is None else total + row_sum
+        acc = term if acc is None else acc + term
+    return best, total, acc
+
+
+def query_rows(q_keep, got, r, i, count):
+    return (q_keep[0, r, i : i + count] + got[0, 1 - r, i : i + count].astype(F32)).astype(BF16)
+
+
+def hold(parts, held, sems):
+    copies = fetch(parts, [held.at[j] for j in range(len(parts))], sems)
     for copy in copies:
         copy.wait()
 
-    def piece(j, side):
-        return held[j, side].reshape(chunk, HEAD_DIM)
-
+
+def attend_early_kernel(where, q_keep, got, *refs):
+    parts, (tops, totals, sums, scores, held, sems) = refs[:-6], refs[-6:]
+    step_rows = scores.shape[0]
+    hold(parts, held, sems)
+    for r in range(2):
+        for i in range(0, q_keep.shape[2], step_rows):
+            best, total, acc = attend_rows(query_rows(q_keep, got, r, i, step_rows), held, scores)
+            tops[r, i : i + step_rows] = jnp.broadcast_to(best, acc.shape)
+            totals[r, i : i + step_rows] = jnp.broadcast_to(total, acc.shape)
+            sums[r, i : i + step_rows] = acc
+
+
+def attend_kernel(where, q_keep, got, tops, totals, sums, part, mine, send, scores, held, sems):
+    scale = HEAD_DIM ** (-0.5)
+    step_rows = scores.shape[0]
+    hold([part], held, sems)
     for r, out in enumerate((mine, send)):
         for i in range(0, q_keep.shape[2], step_rows):
-            query = (q_keep[0, r, i : i + step_rows] + got[0, 1 - r, i : i + step_rows].astype(F32)).astype(BF16)
-            best = None
-            for j in range(count):
-                part = dot_t(query, piece(j, 0))
-                scores[:, j * chunk : (j + 1) * chunk] = part
-                top = jnp.max(part, axis=-1, keepdims=True)
-                best = top if best is None else jnp.maximum(best, top)
-            total = jnp.zeros((step_rows, 1), F32)
-            acc = jnp.zeros((step_rows, HEAD_DIM), F32)
-            for j in range(count):
-                weights = jnp.exp((scores[:, j * chunk : (j + 1) * chunk] - best) * scale)
-                total = total + jnp.sum(weights, axis=-1, keepdims=True)
-                acc = acc + dot(weights.astype(BF16), piece(j, 1))
-            out[i : i + step_rows, :] = (acc / total).astype(BF16)
+            best, total, acc = attend_rows(query_rows(q_keep, got, r, i, step_rows), held, scores)
+            before = tops[r, i : i + step_rows]
+            top = jnp.maximum(before, best)
+            old, new = jnp.exp((before - top) * scale), jnp.exp((best - top) * scale)
+            total = totals[r, i : i + step_rows] * old + total * new
+            out[i : i + step_rows, :] = ((sums[r, i : i + step_rows] * old + acc * new) / total).astype(BF16)
 
 
 def spread_out(inputs, pairs, places, mine, other, same):
@@ -278,12 +323,15 @@
     far = both_ways(r3[:, :half], l3[:, half:])
     swapped, late_far = step((shift(got, "c", 1), late_far))
     late = jnp.stack([late, late_far], axis=1).reshape(6, block, block)
+    sums = run_kernel(
+        project_early_kernel, where, [mine, got, swapped], S((3, 2, rows, block), F32),
+        [pltpu.VMEM((len(EARLY), 3, block, block), BF16), pltpu.SemaphoreType.DMA((len(EARLY),))], 60,
+        4 * rows * width * block, 6 << 20, pinned=[qkv_weight, l1, l2, r2, r1])
     kv_keep, q_keep, send = run_kernel(
-        project_kernel, where, [mine, got, swapped],
+        project_kernel, where, [mine, got, swapped, sums],
         [S((2, 2, rows, HEAD_DIM), F32), S((1, 2, rows, HEAD_DIM), F32), S((3, 2, rows, HEAD_DIM), BF16)],
-        [pltpu.VMEM((3, blocks, block, block), BF16), pltpu.SemaphoreType.DMA((3, 9))], 60,
-        6 * rows * width * block, 6 * block * block * 8 + 4 * rows * width,
-        pinned=[qkv_weight, l1, l2, l3, *far, r3, r2, r1])
+        [pltpu.VMEM((len(LATE), 3, block, block), BF16), pltpu.SemaphoreType.DMA((4,))], 60,
+        2 * rows * width * block, 6 << 20, pinned=[l3, *far, r3])
     got, late = step((shift(send, "xl", 1), late))
     kv = (kv_keep + got[1:, ::-1].astype(F32)).astype(BF16)
 
@@ -293,13 +341,21 @@
     out_weight = [out_weight, shift(out_weight, "xl", 1)]
     kv_r3, kv_l3, late_left = step((kv_r3, kv_l3, late))
     late_l1 = shift(late_left, "z", -1)
-    kv_r4, late_right = step((shift(kv_r3, "z", 1), late))
+    kv_r4 = shift(kv_r3, "z", 1)
+    parts = [kv, kv_l1, kv_l2, kv_l3, kv_r3, kv_r2, kv_r1]
+    stat = S((2, rows, HEAD_DIM), F32)
+
+    def attend_scratch(count):
+        return [pltpu.VMEM((128, 2 * rows * count), F32), pltpu.VMEM((count, 2, 2, rows, HEAD_DIM), BF16), pltpu.SemaphoreType.DMA((count,))]
+
+    tops, totals, sums = run_kernel(
+        attend_early_kernel, where, [q_keep, got], [stat] * 3, attend_scratch(len(parts)), 32,
+        7 * rows * 16 * rows * HEAD_DIM, 4 << 20, 2 * rows * 14 * rows, pinned=parts)
+    kv_r4, late_right, tops, totals, sums = step((kv_r4, late, tops, totals, sums))
     late_r1 = shift(late_right, "z", 1)
     own, away = run_kernel(
-        attend_kernel, where, [q_keep, got], [S((rows, HEAD_DIM), BF16)] * 2,
-        [pltpu.VMEM((128, 16 * rows), F32), pltpu.VMEM((blocks, 2, 2, rows, HEAD_DIM), BF16), pltpu.SemaphoreType.DMA((blocks,))], 32,
-        8 * rows * 16 * rows * HEAD_DIM, 4 << 20, 2 * rows * 16 * rows,
-        pinned=[kv, kv_l1, kv_l2, kv_l3, kv_r4, kv_r3, kv_r2, kv_r1])
+        attend_kernel, where, [q_keep, got, tops, totals, sums], [S((rows, HEAD_DIM), BF16)] * 2, attend_scratch(1), 32,
+        rows * 16 * rows * HEAD_DIM, 2 << 20, 2 * rows * 2 * rows, pinned=[kv_r4])
     back, late_l1 = step((shift(away, "xl", 1), late_l1))
     blocks_out = [S((blocks, rows, block), BF16)] * 2
     mine, other = run_kernel(

time: 235 us -> 236 us (level)
  Pallas kernels: 26.1 us -> 31.7 us
  waiting for transfers between devices: 90.2 us -> 85.1 us
  starting transfers between devices: 73.8 us -> 70.7 us
    pallas_call x7 -> x9, Pallas kernels: 26.1 us -> 31.7 us  [run_kernel(): pl.pallas_call(body, out_shape=outs, in_specs=[smem()] + [vmem()] * len(a...]
    ppermute x33, waiting for transfers between devices: 85.8 us -> 81.2 us  [shift(): lax.ppermute(value, axis, [(i, (i + step) % count) for i in range(count)])]
    ppermute x33, starting transfers between devices: 61.1 us -> 58.1 us  [shift(): lax.ppermute(value, axis, [(i, (i + step) % count) for i in range(count)])]
  transfers between devices with their start and end apart: 36 -> 36, of which waited for: 21 -> 21; matrix products, arithmetic and copies ran while one was open for 1% -> 2% of each run, Pallas kernels for 8% -> 10%
where the time goes in v1:
time: 236 us
  waiting for transfers between devices  85.1 us (36%)
  starting transfers between devices  70.7 us (30%)
  Pallas kernels  31.7 us (13%)
  blocking collectives  22 us (9%)
  between operations  13.7 us (6%)
  local copies, waits for them, and re-layouts  8.44 us (4%)
  other arithmetic  4.33 us (2%)
    ppermute x33, waiting for transfers between devices, shift(): lax.ppermute(value, axis, [(i, (i + step) % count) for i in range(count)])  81.2 us
    ppermute x33, starting transfers between devices, shift(): lax.ppermute(value, axis, [(i, (i + step) % count) for i in range(count)])  58.1 us
    pallas_call x9, Pallas kernels, run_kernel(): pl.pallas_call(body, out_shape=outs, in_specs=[smem()] + [vmem()] * len(a...  31.7 us
    all_to_all x1, blocking collectives, exchange(): return lax.all_to_all(parts, CHIPS, 0, 0, tiled=True)  22 us
    all_to_all x2, starting transfers between devices, exchange(): return lax.all_to_all(parts, CHIPS, 0, 0, tiled=True)  12.6 us
    unnamed x56, local copies, waits for them, and re-layouts  6.81 us
  transfers between devices with their start and end apart: 36, of which 21 were waited for; matrix products, arithmetic and copies ran while one was open for 2% of the time, Pallas kernels for 10%

profile of v1, /device:TPU:1, one launch (start us, length us, event | category | flops | bytes accessed | tf_op | source)
XLA Modules:
  0.0 236.0 jit_solution(7194414095891731553)
XLA Ops:
  6.5 6.4 %collective-permute-start.3 = (bf16[3,256,256]{2,1,0:T(8,128)(2,1)}, bf16[3,256,256]{2,1,0:T(8,128)(2,1)S(1)}, u32[]{:S(2)}, u32[]{:S(2)}) collective-permute-start(bf16[3,256,256]{2,1,0:T(8,128)(2,1)} %refs_0_.1), channel_id=1, source_target_pairs={{0,224},{32,0},{64,32},{96,64},{128,96},{160,128},{192,160},{224,1... | collective-permute-start | bytes 1179656 | tf_op jit(solution)/shard_map/ppermute | solution.py:18
  21.0 3.3 %collective-permute-start.4 = (bf16[3,256,256]{2,1,0:T(8,128)(2,1)S(1)}, bf16[3,256,256]{2,1,0:T(8,128)(2,1)S(1)}, u32[]{:S(2)}, u32[]{:S(2)}) collective-permute-start(bf16[3,256,256]{2,1,0:T(8,128)(2,1)S(1)} %collective-permute-done.3.refs_1_), channel_id=1, source_target_pairs={{0,224},{32,0},{64,32},{96,64},{128,96},{160,128},{192,160},{224,1... | collective-permute-start | bytes 1179656 | tf_op jit(solution)/shard_map/ppermute | solution.py:18
  24.4 7.5 %collective-permute-done.got = bf16[4,256,256]{2,1,0:T(8,128)(2,1)S(1)} collective-permute-done((bf16[4,256,256]{2,1,0:T(8,128)(2,1)S(1)}, bf16[4,256,256]{2,1,0:T(8,128)(2,1)S(1)}, u32[]{:S(2)}, u32[]{:S(2)}) %collective-permute-start) | collective-permute-done | bytes 524320 | tf_op jit(solution)/shard_map/ppermute | solution.py:18
  38.3 6.0 %collective-permute-done.7.refs_0_ = bf16[3,256,256]{2,1,0:T(8,128)(2,1)S(1)} collective-permute-done((bf16[3,256,256]{2,1,0:T(8,128)(2,1)S(1)}, bf16[3,256,256]{2,1,0:T(8,128)(2,1)S(1)}, u32[]{:S(2)}, u32[]{:S(2)}) %collective-permute-start.7) | collective-permute-done | bytes 393248 | tf_op jit(solution)/shard_map/ppermute | solution.py:18
  49.6 5.4 %shard_map.101.sums = f32[3,2,256,256]{3,2,1,0:T(8,128)} custom-call(s32[5]{0:T(128)} %copy-done.8, bf16[8,256,256]{2,1,0:T(8,128)(2,1)} %copy-done.2, bf16[4,256,256]{2,1,0:T(8,128)(2,1)} %copy-done.15, bf16[4,256,256]{2,1,0:T(8,128)(2,1)} %copy-done.16, bf16[3,256,256]{2,1,0:T(8,128)(2,1)} %refs_0_.1, bf16[3,256,256]{2,1,0:T(8,128)(2,1)} %copy-done.21, ...), custom_call_target="tpu_custom_call" | custom-call | flops 1073741824 | bytes 6291456 | tf_op jit(solution)/shard_map/pallas_call | solution.py:34
  55.1 3.3 %collective-permute-done.9.refs_1_ = bf16[3,128,256]{2,1,0:T(8,128)(2,1)S(1)} collective-permute-done((bf16[3,128,256]{2,1,0:T(8,128)(2,1)}, bf16[3,128,256]{2,1,0:T(8,128)(2,1)S(1)}, u32[]{:S(2)}, u32[]{:S(2)}) %collective-permute-start.9) | collective-permute-done | bytes 196640 | tf_op jit(solution)/shard_map/ppermute | solution.py:18
  59.1 5.1 %shard_map.102 = (f32[2,2,256,128]{3,2,1,0:T(8,128)}, f32[1,2,256,128]{3,2,1,0:T(8,128)}, bf16[3,2,256,128]{3,2,1,0:T(8,128)(2,1)}) custom-call(s32[5]{0:T(128)} %copy-done.8, bf16[8,256,256]{2,1,0:T(8,128)(2,1)} %copy-done.2, bf16[4,256,256]{2,1,0:T(8,128)(2,1)} %copy-done.15, bf16[4,256,256]{2,1,0:T(8,128)(2,1)} %copy-done.16, ...), custom_call_target="tpu_custom_call" | custom-call | flops 536870912 | bytes 6291456 | tf_op jit(solution)/shard_map/pallas_call | solution.py:34
  66.6 6.2 %collective-permute-done.11.got = bf16[3,2,256,128]{3,2,1,0:T(8,128)(2,1)S(1)} collective-permute-done((bf16[3,2,256,128]{3,2,1,0:T(8,128)(2,1)}, bf16[3,2,256,128]{3,2,1,0:T(8,128)(2,1)S(1)}, u32[]{:S(2)}, u32[]{:S(2)}) %collective-permute-start.11) | collective-permute-done | bytes 393248 | tf_op jit(solution)/shard_map/ppermute | solution.py:18
  75.7 3.8 %collective-permute-done.12.refs_6_ = bf16[2,2,256,128]{3,2,1,0:T(8,128)(2,1)S(1)} collective-permute-done((bf16[2,2,256,128]{3,2,1,0:T(8,128)(2,1)S(1)}, bf16[2,2,256,128]{3,2,1,0:T(8,128)(2,1)S(1)}, u32[]{:S(2)}, u32[]{:S(2)}) %collective-permute-start.12) | collective-permute-done | bytes 262176 | tf_op jit(solution)/shard_map/ppermute | solution.py:18
  82.2 3.8 %collective-permute-done.13.refs_5_ = bf16[2,2,256,128]{3,2,1,0:T(8,128)(2,1)S(1)} collective-permute-done((bf16[2,2,256,128]{3,2,1,0:T(8,128)(2,1)S(1)}, bf16[2,2,256,128]{3,2,1,0:T(8,128)(2,1)S(1)}, u32[]{:S(2)}, u32[]{:S(2)}) %collective-permute-start.13) | collective-permute-done | bytes 262176 | tf_op jit(solution)/shard_map/ppermute | solution.py:18
  90.0 3.4 %collective-permute-done.14.refs_4_ = bf16[2,2,256,128]{3,2,1,0:T(8,128)(2,1)S(1)} collective-permute-done((bf16[2,2,256,128]{3,2,1,0:T(8,128)(2,1)S(1)}, bf16[2,2,256,128]{3,2,1,0:T(8,128)(2,1)S(1)}, u32[]{:S(2)}, u32[]{:S(2)}) %collective-permute-start.14) | collective-permute-done | bytes 262176 | tf_op jit(solution)/shard_map/ppermute | solution.py:18
  93.4 3.1 %collective-permute-start.20 = (bf16[6,256,256]{2,1,0:T(8,128)(2,1)S(1)}, bf16[6,256,256]{2,1,0:T(8,128)(2,1)}, u32[]{:S(2)}, u32[]{:S(2)}) collective-permute-start(bf16[6,256,256]{2,1,0:T(8,128)(2,1)S(1)} %bitcast.13), channel_id=1, source_target_pairs={{0,224},{32,0},{64,32},{96,64},{128,96},{160,128},{192,160},{224,1... | collective-permute-start | bytes 2359304 | tf_op jit(solution)/shard_map/ppermute | solution.py:18
  96.5 4.3 %shard_map.103 = (f32[2,256,128]{2,1,0:T(8,128)S(1)}, f32[2,256,128]{2,1,0:T(8,128)S(1)}, f32[2,256,128]{2,1,0:T(8,128)S(1)}) custom-call(s32[5]{0:T(128)S(1)} %copy-done.9, f32[1,2,256,128]{3,2,1,0:T(8,128)S(1)} %copy-done.7, bf16[3,2,256,128]{3,2,1,0:T(8,128)(2,1)S(1)} %collective-permute-done.11.got, ...), custom_call_target="tpu_custom_call" | custom-call | flops 939524096 | bytes 4194304 | tf_op jit(solution)/shard_map/pallas_call | solution.py:34
  110.3 6.6 %collective-permute-done.22.refs_7_ = bf16[6,256,256]{2,1,0:T(8,128)(2,1)S(1)} collective-permute-done((bf16[6,256,256]{2,1,0:T(8,128)(2,1)S(1)}, bf16[6,256,256]{2,1,0:T(8,128)(2,1)S(1)}, u32[]{:S(2)}, u32[]{:S(2)}) %collective-permute-start.22) | collective-permute-done | bytes 786464 | tf_op jit(solution)/shard_map/ppermute | solution.py:18
  116.9 9.4 %collective-permute-start.23 = (bf16[8,256,256]{2,1,0:T(8,128)(2,1)S(1)}, bf16[8,256,256]{2,1,0:T(8,128)(2,1)S(1)}, u32[]{:S(2)}, u32[]{:S(2)}) collective-permute-start(bf16[8,256,256]{2,1,0:T(8,128)(2,1)S(1)} %get-tuple-element.67), channel_id=1, source_target_pairs={{0,1},{1,0},{2,3},{3,2},{4,5},{5,4},{6,7},{7,6},{8,9},{9,8},{10,11... | collective-permute-start | bytes 3145736 | tf_op jit(solution)/shard_map/ppermute | solution.py:18
  129.8 7.0 %all-to-all-start = ((bf16[8,256,256]{2,1,0:T(8,128)(2,1)}), bf16[8,256,256]{2,1,0:T(8,128)(2,1)}, u32[]{:S(2)}, u32[]{:S(2)}) async-start(bf16[8,256,256]{2,1,0:T(8,128)(2,1)} %add_convert_fusion.1), calls=%async_computation | async-start | bytes 2097152 | tf_op jit(solution)/shard_map/all_to_all | solution.py:288
  137.0 8.8 %collective-permute-done.24.refs_2_ = bf16[6,256,256]{2,1,0:T(8,128)(2,1)} collective-permute-done((bf16[6,256,256]{2,1,0:T(8,128)(2,1)}, bf16[6,256,256]{2,1,0:T(8,128)(2,1)}, u32[]{:S(2)}, u32[]{:S(2)}) %collective-permute-start.24) | collective-permute-done | bytes 786464 | tf_op jit(solution)/shard_map/ppermute | solution.py:18
  147.6 3.9 %all-to-all-done.parts = bf16[8,256,256]{2,1,0:T(8,128)(2,1)} async-done(((bf16[8,256,256]{2,1,0:T(8,128)(2,1)}), bf16[8,256,256]{2,1,0:T(8,128)(2,1)}, u32[]{:S(2)}, u32[]{:S(2)}) %all-to-all-start) | async-done | bytes 1048608 | tf_op jit(solution)/shard_map/all_to_all | solution.py:288
  155.4 5.6 %all-to-all-start.1 = ((bf16[8,256,256]{2,1,0:T(8,128)(2,1)}), bf16[8,256,256]{2,1,0:T(8,128)(2,1)}, u32[]{:S(2)}, u32[]{:S(2)}) async-start(bf16[8,256,256]{2,1,0:T(8,128)(2,1)} %copy-done.6), calls=%async_computation.1 | async-start | bytes 2097152 | tf_op jit(solution)/shard_map/all_to_all | solution.py:288
  161.1 3.3 %collective-permute-done.25.refs_3_ = bf16[6,256,256]{2,1,0:T(8,128)(2,1)} collective-permute-done((bf16[6,256,256]{2,1,0:T(8,128)(2,1)}, bf16[6,256,256]{2,1,0:T(8,128)(2,1)}, u32[]{:S(2)}, u32[]{:S(2)}) %collective-permute-start.25) | collective-permute-done | bytes 786464 | tf_op jit(solution)/shard_map/ppermute | solution.py:18
  167.4 13.4 %collective-permute-done.28.refs_5_ = bf16[6,256,256]{2,1,0:T(8,128)(2,1)S(1)} collective-permute-done((bf16[6,256,256]{2,1,0:T(8,128)(2,1)}, bf16[6,256,256]{2,1,0:T(8,128)(2,1)S(1)}, u32[]{:S(2)}, u32[]{:S(2)}) %collective-permute-start.28) | collective-permute-done | bytes 786464 | tf_op jit(solution)/shard_map/ppermute | solution.py:18
  189.0 5.4 %shard_map.107.gated = bf16[256,256]{1,0:T(8,128)(2,1)S(1)} custom-call(s32[5]{0:T(128)S(1)} %copy-done.9, bf16[8,256,256]{2,1,0:T(8,128)(2,1)} %all-to-all-done.1.mine, bf16[8,256,256]{2,1,0:T(8,128)(2,1)} %copy-done.17, f32[1,4096]{1,0:T(1,128)S(1)} %bitcast.18, bf16[6,256,256]{2,1,0:T(8,128)(2,1)S(1)} %bitcast.15, ...), custom_call_target="tpu_custom_call" | custom-call | flops 1073741824 | bytes 6291456 | tf_op jit(solution)/shard_map/pallas_call | solution.py:34
  195.6 3.1 %collective-permute-start.31 = (bf16[16,256]{1,0:T(8,128)(2,1)S(1)}, bf16[16,256]{1,0:T(8,128)(2,1)S(1)}, u32[]{:S(2)}, u32[]{:S(2)}) collective-permute-start(bf16[16,256]{1,0:T(8,128)(2,1)S(1)} %get-tuple-element.79), channel_id=1, source_target_pairs={{0,240},{16,0},{32,16},{48,32},{64,48},{80,64},{96,80},{112,96},{1... | collective-permute-start | bytes 24584 | tf_op jit(solution)/shard_map/ppermute | solution.py:18
  206.3 22.0 %all_to_all.15 = bf16[8,256,256]{2,1,0:T(8,128)(2,1)S(1)} all-to-all(bf16[8,256,256]{2,1,0:T(8,128)(2,1)S(1)} %add_convert_fusion), channel_id=1, replica_groups=mesh['z'=8,'xl'=2,'xh'=2,'y'=4,'c'=2] {'xh','y'}, dimensions={0} | all-to-all | bytes 2097152 | tf_op jit(solution)/shard_map/all_to_all | solution.py:288
  (128 shorter events, 72.3 us)
Async XLA Ops:
  6.5 82.3 %all-gather.2.cloned.1.call-start = ((), (), s32[]{:S(2)}) async-start(), calls=%async_computation.3 | async-start | bytes 1179648 | tf_op jit(solution)/shard_map/all_gather | solution.py:311
  6.5 14.5 %collective-permute-start.3 = (bf16[3,256,256]{2,1,0:T(8,128)(2,1)}, bf16[3,256,256]{2,1,0:T(8,128)(2,1)S(1)}, u32[]{:S(2)}, u32[]{:S(2)}) collective-permute-start(bf16[3,256,256]{2,1,0:T(8,128)(2,1)} %refs_0_.1), channel_id=1, source_target_pairs={{0,224},{32,0},{64,32},{96,64},{128,96},{160,128},{192,160},{224,1... | collective-permute-start | bytes 1179656 | tf_op jit(solution)/shard_map/ppermute | solution.py:18
  12.9 11.4 %collective-permute-start.5 = (bf16[3,256,256]{2,1,0:T(8,128)(2,1)}, bf16[3,256,256]{2,1,0:T(8,128)(2,1)S(1)}, u32[]{:S(2)}, u32[]{:S(2)}) collective-permute-start(bf16[3,256,256]{2,1,0:T(8,128)(2,1)} %refs_0_.1), channel_id=1, source_target_pairs={{0,32},{32,64},{64,96},{96,128},{128,160},{160,192},{192,224},{224... | collective-permute-start | bytes 1179656 | tf_op jit(solution)/shard_map/ppermute | solution.py:18
  19.2 12.6 %collective-permute-start = (bf16[4,256,256]{2,1,0:T(8,128)(2,1)S(1)}, bf16[4,256,256]{2,1,0:T(8,128)(2,1)S(1)}, u32[]{:S(2)}, u32[]{:S(2)}) collective-permute-start(bf16[4,256,256]{2,1,0:T(8,128)(2,1)S(1)} %get-tuple-element.42), channel_id=1, source_target_pairs={{0,16},{16,0},{1,17},{17,1},{2,18},{18,2},{3,19},{19,3},{4,20},{20... | collective-permute-start | bytes 1572872 | tf_op jit(solution)/shard_map/ppermute | solution.py:18
  21.0 12.5 %collective-permute-start.4 = (bf16[3,256,256]{2,1,0:T(8,128)(2,1)S(1)}, bf16[3,256,256]{2,1,0:T(8,128)(2,1)S(1)}, u32[]{:S(2)}, u32[]{:S(2)}) collective-permute-start(bf16[3,256,256]{2,1,0:T(8,128)(2,1)S(1)} %collective-permute-done.3.refs_1_), channel_id=1, source_target_pairs={{0,224},{32,0},{64,32},{96,64},{128,96},{160,128},{192,160},{224,1... | collective-permute-start | bytes 1179656 | tf_op jit(solution)/shard_map/ppermute | solution.py:18
  24.4 11.9 %collective-permute-start.6 = (bf16[3,256,256]{2,1,0:T(8,128)(2,1)S(1)}, bf16[3,256,256]{2,1,0:T(8,128)(2,1)}, u32[]{:S(2)}, u32[]{:S(2)}) collective-permute-start(bf16[3,256,256]{2,1,0:T(8,128)(2,1)S(1)} %collective-permute-done.5.refs_4_), channel_id=1, source_target_pairs={{0,32},{32,64},{64,96},{96,128},{128,160},{160,192},{192,224},{224... | collective-permute-start | bytes 1179656 | tf_op jit(solution)/shard_map/ppermute | solution.py:18
  31.8 17.0 %collective-permute-start.1 = (bf16[4,256,256]{2,1,0:T(8,128)(2,1)S(1)}, bf16[4,256,256]{2,1,0:T(8,128)(2,1)S(1)}, u32[]{:S(2)}, u32[]{:S(2)}) collective-permute-start(bf16[4,256,256]{2,1,0:T(8,128)(2,1)S(1)} %collective-permute-done.got), channel_id=1, source_target_pairs={{0,1},{1,0},{2,3},{3,2},{4,5},{5,4},{6,7},{7,6},{8,9},{9,8},{10,11... | collective-permute-start | bytes 1572872 | tf_op jit(solution)/shard_map/ppermute | solution.py:18
  33.6 10.8 %collective-permute-start.7 = (bf16[3,256,256]{2,1,0:T(8,128)(2,1)S(1)}, bf16[3,256,256]{2,1,0:T(8,128)(2,1)S(1)}, u32[]{:S(2)}, u32[]{:S(2)}) collective-permute-start(bf16[3,256,256]{2,1,0:T(8,128)(2,1)S(1)} %collective-permute-done.4.refs_2_), channel_id=1, source_target_pairs={{0,224},{32,0},{64,32},{96,64},{128,96},{160,128},{192,160},{224,1... | collective-permute-start | bytes 1179656 | tf_op jit(solution)/shard_map/ppermute | solution.py:18
  36.3 11.8 %collective-permute-start.8 = (bf16[3,256,256]{2,1,0:T(8,128)(2,1)}, bf16[3,256,256]{2,1,0:T(8,128)(2,1)S(1)}, u32[]{:S(2)}, u32[]{:S(2)}) collective-permute-start(bf16[3,256,256]{2,1,0:T(8,128)(2,1)} %collective-permute-done.6.refs_3_), channel_id=1, source_target_pairs={{0,32},{32,64},{64,96},{96,128},{128,160},{160,192},{192,224},{224... | collective-permute-start | bytes 1179656 | tf_op jit(solution)/shard_map/ppermute | solution.py:18
  37.1 11.7 %collective-permute-start.2 = (bf16[3,256,256]{2,1,0:T(8,128)(2,1)}, bf16[3,256,256]{2,1,0:T(8,128)(2,1)}, u32[]{:S(2)}, u32[]{:S(2)}) collective-permute-start(bf16[3,256,256]{2,1,0:T(8,128)(2,1)} %get-tuple-element.78), channel_id=1, source_target_pairs={{0,16},{16,0},{1,17},{17,1},{2,18},{18,2},{3,19},{19,3},{4,20},{20... | collective-permute-start | bytes 1179656 | tf_op jit(solution)/shard_map/ppermute | solution.py:18
  45.1 9.9 %collective-permute-start.10 = (bf16[3,128,256]{2,1,0:T(8,128)(2,1)}, bf16[3,128,256]{2,1,0:T(8,128)(2,1)S(1)}, u32[]{:S(2)}, u32[]{:S(2)}) collective-permute-start(bf16[3,128,256]{2,1,0:T(8,128)(2,1)} %slice.21), channel_id=1, source_target_pairs={{0,224},{32,0},{64,32},{96,64},{128,96},{160,128},{192,160},{224,1... | collective-permute-start | bytes 589832 | tf_op jit(solution)/shard_map/ppermute | solution.py:18
  48.8 9.6 %collective-permute-start.9 = (bf16[3,128,256]{2,1,0:T(8,128)(2,1)}, bf16[3,128,256]{2,1,0:T(8,128)(2,1)S(1)}, u32[]{:S(2)}, u32[]{:S(2)}) collective-permute-start(bf16[3,128,256]{2,1,0:T(8,128)(2,1)} %slice.20), channel_id=1, source_target_pairs={{0,32},{32,64},{64,96},{96,128},{128,160},{160,192},{192,224},{224... | collective-permute-start | bytes 589832 | tf_op jit(solution)/shard_map/ppermute | solution.py:18
  64.1 8.7 %collective-permute-start.11 = (bf16[3,2,256,128]{3,2,1,0:T(8,128)(2,1)}, bf16[3,2,256,128]{3,2,1,0:T(8,128)(2,1)S(1)}, u32[]{:S(2)}, u32[]{:S(2)}) collective-permute-start(bf16[3,2,256,128]{3,2,1,0:T(8,128)(2,1)} %get-tuple-element.45), channel_id=1, source_target_pairs={{0,16},{16,0},{1,17},{17,1},{2,18},{18,2},{3,19},{19,3},{4,20},{20... | collective-permute-start | bytes 1179656 | tf_op jit(solution)/shard_map/ppermute | solution.py:18
  88.8 20.2 %collective-permute-start.21 = (bf16[2048,256]{1,0:T(8,128)(2,1)}, bf16[2048,256]{1,0:T(8,128)(2,1)S(1)}, u32[]{:S(2)}, u32[]{:S(2)}) collective-permute-start(bf16[2048,256]{1,0:T(8,128)(2,1)} %all-gather.2.cloned.1.call-done.weight), channel_id=1, source_target_pairs={{0,16},{16,0},{1,17},{17,1},{2,18},{18,2},{3,19},{19,3},{4,20},{20... | collective-permute-start | bytes 3145736 | tf_op jit(solution)/shard_map/ppermute | solution.py:18
  93.4 15.5 %collective-permute-start.20 = (bf16[6,256,256]{2,1,0:T(8,128)(2,1)S(1)}, bf16[6,256,256]{2,1,0:T(8,128)(2,1)}, u32[]{:S(2)}, u32[]{:S(2)}) collective-permute-start(bf16[6,256,256]{2,1,0:T(8,128)(2,1)S(1)} %bitcast.13), channel_id=1, source_target_pairs={{0,224},{32,0},{64,32},{96,64},{128,96},{160,128},{192,160},{224,1... | collective-permute-start | bytes 2359304 | tf_op jit(solution)/shard_map/ppermute | solution.py:18
  102.0 14.9 %collective-permute-start.22 = (bf16[6,256,256]{2,1,0:T(8,128)(2,1)S(1)}, bf16[6,256,256]{2,1,0:T(8,128)(2,1)S(1)}, u32[]{:S(2)}, u32[]{:S(2)}) collective-permute-start(bf16[6,256,256]{2,1,0:T(8,128)(2,1)S(1)} %bitcast.14), channel_id=1, source_target_pairs={{0,32},{32,64},{64,96},{96,128},{128,160},{160,192},{192,224},{224... | collective-permute-start | bytes 2359304 | tf_op jit(solution)/shard_map/ppermute | solution.py:18
  116.9 11.7 %collective-permute-start.23 = (bf16[8,256,256]{2,1,0:T(8,128)(2,1)S(1)}, bf16[8,256,256]{2,1,0:T(8,128)(2,1)S(1)}, u32[]{:S(2)}, u32[]{:S(2)}) collective-permute-start(bf16[8,256,256]{2,1,0:T(8,128)(2,1)S(1)} %get-tuple-element.67), channel_id=1, source_target_pairs={{0,1},{1,0},{2,3},{3,2},{4,5},{5,4},{6,7},{7,6},{8,9},{9,8},{10,11... | collective-permute-start | bytes 3145736 | tf_op jit(solution)/shard_map/ppermute | solution.py:18
  126.3 19.5 %collective-permute-start.24 = (bf16[6,256,256]{2,1,0:T(8,128)(2,1)}, bf16[6,256,256]{2,1,0:T(8,128)(2,1)}, u32[]{:S(2)}, u32[]{:S(2)}) collective-permute-start(bf16[6,256,256]{2,1,0:T(8,128)(2,1)} %collective-permute-done.20.refs_1_), channel_id=1, source_target_pairs={{0,224},{32,0},{64,32},{96,64},{128,96},{160,128},{192,160},{224,1... | collective-permute-start | bytes 2359304 | tf_op jit(solution)/shard_map/ppermute | solution.py:18
  129.8 21.6 %all-to-all-start = ((bf16[8,256,256]{2,1,0:T(8,128)(2,1)}), bf16[8,256,256]{2,1,0:T(8,128)(2,1)}, u32[]{:S(2)}, u32[]{:S(2)}) async-start(bf16[8,256,256]{2,1,0:T(8,128)(2,1)} %add_convert_fusion.1), calls=%async_computation | async-start | bytes 2097152 | tf_op jit(solution)/shard_map/all_to_all | solution.py:288
  136.9 24.1 %collective-permute-start.27 = (bf16[6,256,256]{2,1,0:T(8,128)(2,1)}, bf16[6,256,256]{2,1,0:T(8,128)(2,1)}, u32[]{:S(2)}, u32[]{:S(2)}) collective-permute-start(bf16[6,256,256]{2,1,0:T(8,128)(2,1)} %copy-done.3), channel_id=1, source_target_pairs={{0,32},{32,64},{64,96},{96,128},{128,160},{160,192},{192,224},{224... | collective-permute-start | bytes 2359304 | tf_op jit(solution)/shard_map/ppermute | solution.py:18
  145.8 18.6 %collective-permute-start.25 = (bf16[6,256,256]{2,1,0:T(8,128)(2,1)}, bf16[6,256,256]{2,1,0:T(8,128)(2,1)}, u32[]{:S(2)}, u32[]{:S(2)}) collective-permute-start(bf16[6,256,256]{2,1,0:T(8,128)(2,1)} %collective-permute-done.24.refs_2_), channel_id=1, source_target_pairs={{0,224},{32,0},{64,32},{96,64},{128,96},{160,128},{192,160},{224,1... | collective-permute-start | bytes 2359304 | tf_op jit(solution)/shard_map/ppermute | solution.py:18
  155.4 27.5 %all-to-all-start.1 = ((bf16[8,256,256]{2,1,0:T(8,128)(2,1)}), bf16[8,256,256]{2,1,0:T(8,128)(2,1)}, u32[]{:S(2)}, u32[]{:S(2)}) async-start(bf16[8,256,256]{2,1,0:T(8,128)(2,1)} %copy-done.6), calls=%async_computation.1 | async-start | bytes 2097152 | tf_op jit(solution)/shard_map/all_to_all | solution.py:288
  161.0 19.8 %collective-permute-start.28 = (bf16[6,256,256]{2,1,0:T(8,128)(2,1)}, bf16[6,256,256]{2,1,0:T(8,128)(2,1)S(1)}, u32[]{:S(2)}, u32[]{:S(2)}) collective-permute-start(bf16[6,256,256]{2,1,0:T(8,128)(2,1)} %collective-permute-done.27.refs_6_), channel_id=1, source_target_pairs={{0,32},{32,64},{64,96},{96,128},{128,160},{160,192},{192,224},{224... | collective-permute-start | bytes 2359304 | tf_op jit(solution)/shard_map/ppermute | solution.py:18
  164.4 18.5 %collective-permute-start.26 = (bf16[6,256,256]{2,1,0:T(8,128)(2,1)}, bf16[6,256,256]{2,1,0:T(8,128)(2,1)S(1)}, u32[]{:S(2)}, u32[]{:S(2)}) collective-permute-start(bf16[6,256,256]{2,1,0:T(8,128)(2,1)} %collective-permute-done.25.refs_3_), channel_id=1, source_target_pairs={{0,224},{32,0},{64,32},{96,64},{128,96},{160,128},{192,160},{224,1... | collective-permute-start | bytes 2359304 | tf_op jit(solution)/shard_map/ppermute | solution.py:18
  (40 other events, 474.9 us)
Sparse Core Ops, SparseCore 0:
  38.5 34.4 all-gather.1

commit v2 on v1

--- a/solution.py
+++ b/solution.py
@@ -81,44 +81,24 @@
     lax.fori_loop(0, rows // step_rows, chunk, 0)
 
 
-def both_rows(mine, got, swapped, core):
+def project_kernel(where, mine, got, swapped, *refs):
+    pieces, (kv_keep, q_keep, send, weights, sems) = refs[:-5], refs[-5:]
+    xl, core = where[1], where[2]
     low = [jnp.where(core == 0, got[j], swapped[j]) for j in range(4)]
     high = [jnp.where(core == 0, swapped[j], got[j]) for j in range(4)]
-    return mine, low + high
-
-
-EARLY = (0, 1, 2, 6, 7)
-LATE = (3, 4, 5)
-
-
-def project_early_kernel(where, mine, got, swapped, *refs):
-    pieces, (sums, weights, sems) = refs[:-3], refs[-3:]
-    copies = fetch(pieces, [weights.at[n] for n in range(len(pieces))], sems)
-    sides = both_rows(mine, got, swapped, where[2])
-    for copy in copies:
-        copy.wait()
-    for m in range(3):
-        for r, a in enumerate(sides):
+    half = pieces[4].shape[1]
+    places = [weights.at[:, j] for j in range(4)] + [weights.at[:, 4, :half], weights.at[:, 4, half:]] + [weights.at[:, j] for j in range(5, 8)]
+    copies = {}
+    for m in (1, 2, 0):
+        copies[m] = fetch([piece.at[m] for piece in pieces], [place.at[m] for place in places], sems.at[m])
+    for m, keep, at in ((1, kv_keep, 0), (2, kv_keep, 1), (0, q_keep, 0)):
+        for copy in copies[m]:
+            copy.wait()
+        for r, a in enumerate((mine, low + high)):
             acc = None
-            for n, j in enumerate(EARLY):
-                term = dot(a[j], weights[n, m])
+            for j in range(8):
+                term = dot(a[j], weights[m, j])
                 acc = term if acc is None else acc + term
-            sums[m, r] = acc
-
-
-def project_kernel(where, mine, got, swapped, sums, *refs):
-    pieces, (kv_keep, q_keep, send, weights, sems) = refs[:-5], refs[-5:]
-    xl, core = where[1], where[2]
-    half = pieces[1].shape[1]
-    copies = fetch(pieces, [weights.at[0], weights.at[1, :, :half], weights.at[1, :, half:], weights.at[2]], sems)
-    sides = both_rows(mine, got, swapped, core)
-    for copy in copies:
-        copy.wait()
-    for m, keep, at in ((1, kv_keep, 0), (2, kv_keep, 1), (0, q_keep, 0)):
-        for r, a in enumerate(sides):
-            acc = sums[m, r]
-            for n, j in enumerate(LATE):
-                acc = acc + dot(a[j], weights[n, m])
             even, odd = acc[:, :HEAD_DIM], acc[:, HEAD_DIM:]
             keep[at, r] = jnp.where(xl == 0, even, odd)
             send[m, r] = jnp.where(xl == 0, odd, even).astype(BF16)
@@ -323,15 +303,12 @@
     far = both_ways(r3[:, :half], l3[:, half:])
     swapped, late_far = step((shift(got, "c", 1), late_far))
     late = jnp.stack([late, late_far], axis=1).reshape(6, block, block)
-    sums = run_kernel(
-        project_early_kernel, where, [mine, got, swapped], S((3, 2, rows, block), F32),
-        [pltpu.VMEM((len(EARLY), 3, block, block), BF16), pltpu.SemaphoreType.DMA((len(EARLY),))], 60,
-        4 * rows * width * block, 6 << 20, pinned=[qkv_weight, l1, l2, r2, r1])
     kv_keep, q_keep, send = run_kernel(
-        project_kernel, where, [mine, got, swapped, sums],
+        project_kernel, where, [mine, got, swapped],
         [S((2, 2, rows, HEAD_DIM), F32), S((1, 2, rows, HEAD_DIM), F32), S((3, 2, rows, HEAD_DIM), BF16)],
-        [pltpu.VMEM((len(LATE), 3, block, block), BF16), pltpu.SemaphoreType.DMA((4,))], 60,
-        2 * rows * width * block, 6 << 20, pinned=[l3, *far, r3])
+        [pltpu.VMEM((3, blocks, block, block), BF16), pltpu.SemaphoreType.DMA((3, 9))], 60,
+        6 * rows * width * block, 6 * block * block * 8 + 4 * rows * width,
+        pinned=[qkv_weight, l1, l2, l3, *far, r3, r2, r1])
     got, late = step((shift(send, "xl", 1), late))
     kv = (kv_keep + got[1:, ::-1].astype(F32)).astype(BF16)
 
@@ -361,7 +338,7 @@
     mine, other = run_kernel(
         project_out_kernel, where, [own, back] + out_weight, blocks_out, [], 16,
         2 * rows * block * width, 4 << 20)
-    other, late_r1, late_l1 = step((other, late_r1, late_l1))
+    other, late_r1 = step((other, late_r1))
     late_r2, late_l2 = both_ways(late_r1, late_l1)
     late_r3, late_l3 = both_ways(late_r2, late_l2)
     mixed, copies = run_kernel(

time: 236 us -> 235 us (level)
  Pallas kernels: 31.7 us -> 27.3 us
  waiting for transfers between devices: 85.1 us -> 89.4 us
  starting transfers between devices: 70.7 us -> 73.9 us
    pallas_call x9 -> x8, Pallas kernels: 31.7 us -> 27.3 us  [run_kernel(): pl.pallas_call(body, out_shape=outs, in_specs=[smem()] + [vmem()] * len(a...]
    ppermute x33, waiting for transfers between devices: 81.2 us -> 85.1 us  [shift(): lax.ppermute(value, axis, [(i, (i + step) % count) for i in range(count)])]
    ppermute x33, starting transfers between devices: 58.1 us -> 61.2 us  [shift(): lax.ppermute(value, axis, [(i, (i + step) % count) for i in range(count)])]
  transfers between devices with their start and end apart: 36 -> 36, of which waited for: 21 -> 21; matrix products, arithmetic and copies ran while one was open for 2% -> 1% of each run, Pallas kernels for 10% -> 8%
where the time goes in v2:
time: 235 us
  waiting for transfers between devices  89.4 us (38%)
  starting transfers between devices  73.9 us (31%)
  Pallas kernels  27.3 us (12%)
  blocking collectives  22 us (9%)
  between operations  13.7 us (6%)
  local copies, waits for them, and re-layouts  6.19 us (3%)
  other arithmetic  2.53 us (1%)
    ppermute x33, waiting for transfers between devices, shift(): lax.ppermute(value, axis, [(i, (i + step) % count) for i in range(count)])  85.1 us
    ppermute x33, starting transfers between devices, shift(): lax.ppermute(value, axis, [(i, (i + step) % count) for i in range(count)])  61.2 us
    pallas_call x8, Pallas kernels, run_kernel(): pl.pallas_call(body, out_shape=outs, in_specs=[smem()] + [vmem()] * len(a...  27.3 us
    all_to_all x1, blocking collectives, exchange(): return lax.all_to_all(parts, CHIPS, 0, 0, tiled=True)  22 us
    all_to_all x2, starting transfers between devices, exchange(): return lax.all_to_all(parts, CHIPS, 0, 0, tiled=True)  12.7 us
    unnamed x56, local copies, waits for them, and re-layouts  6 us
  transfers between devices with their start and end apart: 36, of which 21 were waited for; matrix products, arithmetic and copies ran while one was open for 1% of the time, Pallas kernels for 8%

profile of v2, /device:TPU:1, one launch (start us, length us, event | category | flops | bytes accessed | tf_op | source)
XLA Modules:
  0.0 235.0 jit_solution(6070485386651812381)
XLA Ops:
  6.5 6.4 %collective-permute-start.3 = (bf16[3,256,256]{2,1,0:T(8,128)(2,1)}, bf16[3,256,256]{2,1,0:T(8,128)(2,1)S(1)}, u32[]{:S(2)}, u32[]{:S(2)}) collective-permute-start(bf16[3,256,256]{2,1,0:T(8,128)(2,1)} %refs_0_.1), channel_id=1, source_target_pairs={{0,224},{32,0},{64,32},{96,64},{128,96},{160,128},{192,160},{224,1... | collective-permute-start | bytes 1179656 | tf_op jit(solution)/shard_map/ppermute | solution.py:18
  21.0 3.3 %collective-permute-start.4 = (bf16[3,256,256]{2,1,0:T(8,128)(2,1)S(1)}, bf16[3,256,256]{2,1,0:T(8,128)(2,1)S(1)}, u32[]{:S(2)}, u32[]{:S(2)}) collective-permute-start(bf16[3,256,256]{2,1,0:T(8,128)(2,1)S(1)} %collective-permute-done.3.refs_1_), channel_id=1, source_target_pairs={{0,224},{32,0},{64,32},{96,64},{128,96},{160,128},{192,160},{224,1... | collective-permute-start | bytes 1179656 | tf_op jit(solution)/shard_map/ppermute | solution.py:18
  24.4 6.8 %collective-permute-done.4.refs_2_ = bf16[3,256,256]{2,1,0:T(8,128)(2,1)S(1)} collective-permute-done((bf16[3,256,256]{2,1,0:T(8,128)(2,1)S(1)}, bf16[3,256,256]{2,1,0:T(8,128)(2,1)S(1)}, u32[]{:S(2)}, u32[]{:S(2)}) %collective-permute-start.4) | collective-permute-done | bytes 393248 | tf_op jit(solution)/shard_map/ppermute | solution.py:18
  31.2 3.4 %collective-permute-start.5 = (bf16[3,256,256]{2,1,0:T(8,128)(2,1)S(1)}, bf16[3,256,256]{2,1,0:T(8,128)(2,1)S(1)}, u32[]{:S(2)}, u32[]{:S(2)}) collective-permute-start(bf16[3,256,256]{2,1,0:T(8,128)(2,1)S(1)} %collective-permute-done.4.refs_2_), channel_id=1, source_target_pairs={{0,224},{32,0},{64,32},{96,64},{128,96},{160,128},{192,160},{224,1... | collective-permute-start | bytes 1179656 | tf_op jit(solution)/shard_map/ppermute | solution.py:18
  40.6 3.5 %collective-permute-start.10 = (bf16[3,128,256]{2,1,0:T(8,128)(2,1)S(1)}, bf16[3,128,256]{2,1,0:T(8,128)(2,1)S(1)}, u32[]{:S(2)}, u32[]{:S(2)}) collective-permute-start(bf16[3,128,256]{2,1,0:T(8,128)(2,1)S(1)} %slice.21), channel_id=1, source_target_pairs={{0,224},{32,0},{64,32},{96,64},{128,96},{160,128},{192,160},{224,1... | collective-permute-start | bytes 589832 | tf_op jit(solution)/shard_map/ppermute | solution.py:18
  44.2 4.2 %collective-permute-done.2 = bf16[3,256,256]{2,1,0:T(8,128)(2,1)S(1)} collective-permute-done((bf16[3,256,256]{2,1,0:T(8,128)(2,1)S(1)}, bf16[3,256,256]{2,1,0:T(8,128)(2,1)S(1)}, u32[]{:S(2)}, u32[]{:S(2)}) %collective-permute-start.2) | collective-permute-done | bytes 393248 | tf_op jit(solution)/shard_map/ppermute | solution.py:18
  50.6 6.0 %shard_map.101 = (f32[2,2,256,128]{3,2,1,0:T(8,128)}, f32[1,2,256,128]{3,2,1,0:T(8,128)}, bf16[3,2,256,128]{3,2,1,0:T(8,128)(2,1)}) custom-call(s32[5]{0:T(128)} %copy-done.8, bf16[8,256,256]{2,1,0:T(8,128)(2,1)} %copy-done.14, bf16[4,256,256]{2,1,0:T(8,128)(2,1)} %copy-done.21, bf16[4,256,256]{2,1,0:T(8,128)(2,1)} %copy-done.22, ...), custom_call_target="tpu_custom_call" | custom-call | flops 1610612736 | bytes 7340032 | tf_op jit(solution)/shard_map/pallas_call | solution.py:34
  58.1 5.9 %collective-permute-done.11.got = bf16[3,2,256,128]{3,2,1,0:T(8,128)(2,1)S(1)} collective-permute-done((bf16[3,2,256,128]{3,2,1,0:T(8,128)(2,1)}, bf16[3,2,256,128]{3,2,1,0:T(8,128)(2,1)S(1)}, u32[]{:S(2)}, u32[]{:S(2)}) %collective-permute-start.11) | collective-permute-done | bytes 393248 | tf_op jit(solution)/shard_map/ppermute | solution.py:18
  66.8 6.1 %collective-permute-done.12.refs_6_ = bf16[2,2,256,128]{3,2,1,0:T(8,128)(2,1)S(1)} collective-permute-done((bf16[2,2,256,128]{3,2,1,0:T(8,128)(2,1)S(1)}, bf16[2,2,256,128]{3,2,1,0:T(8,128)(2,1)S(1)}, u32[]{:S(2)}, u32[]{:S(2)}) %collective-permute-start.12) | collective-permute-done | bytes 262176 | tf_op jit(solution)/shard_map/ppermute | solution.py:18
  75.6 5.8 %collective-permute-done.13.refs_5_ = bf16[2,2,256,128]{3,2,1,0:T(8,128)(2,1)S(1)} collective-permute-done((bf16[2,2,256,128]{3,2,1,0:T(8,128)(2,1)S(1)}, bf16[2,2,256,128]{3,2,1,0:T(8,128)(2,1)S(1)}, u32[]{:S(2)}, u32[]{:S(2)}) %collective-permute-start.13) | collective-permute-done | bytes 262176 | tf_op jit(solution)/shard_map/ppermute | solution.py:18
  85.6 5.0 %collective-permute-done.14.refs_4_ = bf16[2,2,256,128]{3,2,1,0:T(8,128)(2,1)S(1)} collective-permute-done((bf16[2,2,256,128]{3,2,1,0:T(8,128)(2,1)S(1)}, bf16[2,2,256,128]{3,2,1,0:T(8,128)(2,1)S(1)}, u32[]{:S(2)}, u32[]{:S(2)}) %collective-permute-start.14) | collective-permute-done | bytes 262176 | tf_op jit(solution)/shard_map/ppermute | solution.py:18
  93.3 4.3 %shard_map.102 = (f32[2,256,128]{2,1,0:T(8,128)S(1)}, f32[2,256,128]{2,1,0:T(8,128)S(1)}, f32[2,256,128]{2,1,0:T(8,128)S(1)}) custom-call(s32[5]{0:T(128)S(1)} %copy-done.9, f32[1,2,256,128]{3,2,1,0:T(8,128)S(1)} %copy-done.6, bf16[3,2,256,128]{3,2,1,0:T(8,128)(2,1)S(1)} %collective-permute-done.11.got, ...), custom_call_target="tpu_custom_call" | custom-call | flops 939524096 | bytes 4194304 | tf_op jit(solution)/shard_map/pallas_call | solution.py:34
  101.6 3.5 %collective-permute-done.19.got = bf16[256,128]{1,0:T(8,128)(2,1)S(1)} collective-permute-done((bf16[256,128]{1,0:T(8,128)(2,1)S(1)}, bf16[256,128]{1,0:T(8,128)(2,1)S(1)}, u32[]{:S(2)}, u32[]{:S(2)}) %collective-permute-start.19) | collective-permute-done | bytes 65568 | tf_op jit(solution)/shard_map/ppermute | solution.py:18
  106.4 7.3 %collective-permute-done.22.refs_7_ = bf16[6,256,256]{2,1,0:T(8,128)(2,1)S(1)} collective-permute-done((bf16[6,256,256]{2,1,0:T(8,128)(2,1)S(1)}, bf16[6,256,256]{2,1,0:T(8,128)(2,1)S(1)}, u32[]{:S(2)}, u32[]{:S(2)}) %collective-permute-start.22) | collective-permute-done | bytes 786464 | tf_op jit(solution)/shard_map/ppermute | solution.py:18
  113.8 11.7 %collective-permute-start.23 = (bf16[8,256,256]{2,1,0:T(8,128)(2,1)S(1)}, bf16[8,256,256]{2,1,0:T(8,128)(2,1)S(1)}, u32[]{:S(2)}, u32[]{:S(2)}) collective-permute-start(bf16[8,256,256]{2,1,0:T(8,128)(2,1)S(1)} %get-tuple-element.65), channel_id=1, source_target_pairs={{0,1},{1,0},{2,3},{3,2},{4,5},{5,4},{6,7},{7,6},{8,9},{9,8},{10,11... | collective-permute-start | bytes 3145736 | tf_op jit(solution)/shard_map/ppermute | solution.py:18
  129.1 7.1 %all-to-all-start = ((bf16[8,256,256]{2,1,0:T(8,128)(2,1)}), bf16[8,256,256]{2,1,0:T(8,128)(2,1)}, u32[]{:S(2)}, u32[]{:S(2)}) async-start(bf16[8,256,256]{2,1,0:T(8,128)(2,1)} %add_convert_fusion.1), calls=%async_computation | async-start | bytes 2097152 | tf_op jit(solution)/shard_map/all_to_all | solution.py:268
  136.2 8.8 %collective-permute-done.24.refs_2_ = bf16[6,256,256]{2,1,0:T(8,128)(2,1)} collective-permute-done((bf16[6,256,256]{2,1,0:T(8,128)(2,1)}, bf16[6,256,256]{2,1,0:T(8,128)(2,1)}, u32[]{:S(2)}, u32[]{:S(2)}) %collective-permute-start.24) | collective-permute-done | bytes 786464 | tf_op jit(solution)/shard_map/ppermute | solution.py:18
  146.5 4.3 %all-to-all-done.parts = bf16[8,256,256]{2,1,0:T(8,128)(2,1)} async-done(((bf16[8,256,256]{2,1,0:T(8,128)(2,1)}), bf16[8,256,256]{2,1,0:T(8,128)(2,1)}, u32[]{:S(2)}, u32[]{:S(2)}) %all-to-all-start) | async-done | bytes 1048608 | tf_op jit(solution)/shard_map/all_to_all | solution.py:268
  154.7 5.6 %all-to-all-start.1 = ((bf16[8,256,256]{2,1,0:T(8,128)(2,1)}), bf16[8,256,256]{2,1,0:T(8,128)(2,1)}, u32[]{:S(2)}, u32[]{:S(2)}) async-start(bf16[8,256,256]{2,1,0:T(8,128)(2,1)} %copy-done.5), calls=%async_computation.1 | async-start | bytes 2097152 | tf_op jit(solution)/shard_map/all_to_all | solution.py:268
  160.4 3.2 %collective-permute-done.25.refs_3_ = bf16[6,256,256]{2,1,0:T(8,128)(2,1)} collective-permute-done((bf16[6,256,256]{2,1,0:T(8,128)(2,1)}, bf16[6,256,256]{2,1,0:T(8,128)(2,1)}, u32[]{:S(2)}, u32[]{:S(2)}) %collective-permute-start.25) | collective-permute-done | bytes 786464 | tf_op jit(solution)/shard_map/ppermute | solution.py:18
  166.3 13.8 %collective-permute-done.28.refs_5_ = bf16[6,256,256]{2,1,0:T(8,128)(2,1)S(1)} collective-permute-done((bf16[6,256,256]{2,1,0:T(8,128)(2,1)}, bf16[6,256,256]{2,1,0:T(8,128)(2,1)S(1)}, u32[]{:S(2)}, u32[]{:S(2)}) %collective-permute-start.28) | collective-permute-done | bytes 786464 | tf_op jit(solution)/shard_map/ppermute | solution.py:18
  187.9 5.4 %shard_map.106.gated = bf16[256,256]{1,0:T(8,128)(2,1)S(1)} custom-call(s32[5]{0:T(128)S(1)} %copy-done.9, bf16[8,256,256]{2,1,0:T(8,128)(2,1)} %all-to-all-done.1.mine, bf16[8,256,256]{2,1,0:T(8,128)(2,1)} %copy-done.15, f32[1,4096]{1,0:T(1,128)S(1)} %bitcast.18, bf16[6,256,256]{2,1,0:T(8,128)(2,1)S(1)} %bitcast.15, ...), custom_call_target="tpu_custom_call" | custom-call | flops 1073741824 | bytes 6291456 | tf_op jit(solution)/shard_map/pallas_call | solution.py:34
  194.7 3.1 %collective-permute-start.31 = (bf16[16,256]{1,0:T(8,128)(2,1)S(1)}, bf16[16,256]{1,0:T(8,128)(2,1)S(1)}, u32[]{:S(2)}, u32[]{:S(2)}) collective-permute-start(bf16[16,256]{1,0:T(8,128)(2,1)S(1)} %get-tuple-element.77), channel_id=1, source_target_pairs={{0,240},{16,0},{32,16},{48,32},{64,48},{80,64},{96,80},{112,96},{1... | collective-permute-start | bytes 24584 | tf_op jit(solution)/shard_map/ppermute | solution.py:18
  205.4 22.0 %all_to_all.15 = bf16[8,256,256]{2,1,0:T(8,128)(2,1)S(1)} all-to-all(bf16[8,256,256]{2,1,0:T(8,128)(2,1)S(1)} %add_convert_fusion), channel_id=1, replica_groups=mesh['z'=8,'xl'=2,'xh'=2,'y'=4,'c'=2] {'xh','y'}, dimensions={0} | all-to-all | bytes 2097152 | tf_op jit(solution)/shard_map/all_to_all | solution.py:268
  (127 shorter events, 64.8 us)
Async XLA Ops:
  6.5 77.7 %all-gather.2.cloned.1.call-start = ((), (), s32[]{:S(2)}) async-start(), calls=%async_computation.3 | async-start | bytes 1179648 | tf_op jit(solution)/shard_map/all_gather | solution.py:291
  6.5 14.5 %collective-permute-start.3 = (bf16[3,256,256]{2,1,0:T(8,128)(2,1)}, bf16[3,256,256]{2,1,0:T(8,128)(2,1)S(1)}, u32[]{:S(2)}, u32[]{:S(2)}) collective-permute-start(bf16[3,256,256]{2,1,0:T(8,128)(2,1)} %refs_0_.1), channel_id=1, source_target_pairs={{0,224},{32,0},{64,32},{96,64},{128,96},{160,128},{192,160},{224,1... | collective-permute-start | bytes 1179656 | tf_op jit(solution)/shard_map/ppermute | solution.py:18
  12.9 11.4 %collective-permute-start.6 = (bf16[3,256,256]{2,1,0:T(8,128)(2,1)}, bf16[3,256,256]{2,1,0:T(8,128)(2,1)S(1)}, u32[]{:S(2)}, u32[]{:S(2)}) collective-permute-start(bf16[3,256,256]{2,1,0:T(8,128)(2,1)} %refs_0_.1), channel_id=1, source_target_pairs={{0,32},{32,64},{64,96},{96,128},{128,160},{160,192},{192,224},{224... | collective-permute-start | bytes 1179656 | tf_op jit(solution)/shard_map/ppermute | solution.py:18
  19.2 15.4 %collective-permute-start = (bf16[4,256,256]{2,1,0:T(8,128)(2,1)S(1)}, bf16[4,256,256]{2,1,0:T(8,128)(2,1)S(1)}, u32[]{:S(2)}, u32[]{:S(2)}) collective-permute-start(bf16[4,256,256]{2,1,0:T(8,128)(2,1)S(1)} %get-tuple-element.41), channel_id=1, source_target_pairs={{0,16},{16,0},{1,17},{17,1},{2,18},{18,2},{3,19},{19,3},{4,20},{20... | collective-permute-start | bytes 1572872 | tf_op jit(solution)/shard_map/ppermute | solution.py:18
  21.0 10.2 %collective-permute-start.4 = (bf16[3,256,256]{2,1,0:T(8,128)(2,1)S(1)}, bf16[3,256,256]{2,1,0:T(8,128)(2,1)S(1)}, u32[]{:S(2)}, u32[]{:S(2)}) collective-permute-start(bf16[3,256,256]{2,1,0:T(8,128)(2,1)S(1)} %collective-permute-done.3.refs_1_), channel_id=1, source_target_pairs={{0,224},{32,0},{64,32},{96,64},{128,96},{160,128},{192,160},{224,1... | collective-permute-start | bytes 1179656 | tf_op jit(solution)/shard_map/ppermute | solution.py:18
  24.4 10.3 %collective-permute-start.7 = (bf16[3,256,256]{2,1,0:T(8,128)(2,1)S(1)}, bf16[3,256,256]{2,1,0:T(8,128)(2,1)}, u32[]{:S(2)}, u32[]{:S(2)}) collective-permute-start(bf16[3,256,256]{2,1,0:T(8,128)(2,1)S(1)} %collective-permute-done.6.refs_8_), channel_id=1, source_target_pairs={{0,32},{32,64},{64,96},{96,128},{128,160},{160,192},{192,224},{224... | collective-permute-start | bytes 1179656 | tf_op jit(solution)/shard_map/ppermute | solution.py:18
  31.2 9.4 %collective-permute-start.5 = (bf16[3,256,256]{2,1,0:T(8,128)(2,1)S(1)}, bf16[3,256,256]{2,1,0:T(8,128)(2,1)S(1)}, u32[]{:S(2)}, u32[]{:S(2)}) collective-permute-start(bf16[3,256,256]{2,1,0:T(8,128)(2,1)S(1)} %collective-permute-done.4.refs_2_), channel_id=1, source_target_pairs={{0,224},{32,0},{64,32},{96,64},{128,96},{160,128},{192,160},{224,1... | collective-permute-start | bytes 1179656 | tf_op jit(solution)/shard_map/ppermute | solution.py:18
  34.6 9.4 %collective-permute-start.8 = (bf16[3,256,256]{2,1,0:T(8,128)(2,1)}, bf16[3,256,256]{2,1,0:T(8,128)(2,1)S(1)}, u32[]{:S(2)}, u32[]{:S(2)}) collective-permute-start(bf16[3,256,256]{2,1,0:T(8,128)(2,1)} %collective-permute-done.7.refs_7_), channel_id=1, source_target_pairs={{0,32},{32,64},{64,96},{96,128},{128,160},{160,192},{192,224},{224... | collective-permute-start | bytes 1179656 | tf_op jit(solution)/shard_map/ppermute | solution.py:18
  34.7 13.7 %collective-permute-start.1 = (bf16[4,256,256]{2,1,0:T(8,128)(2,1)S(1)}, bf16[4,256,256]{2,1,0:T(8,128)(2,1)S(1)}, u32[]{:S(2)}, u32[]{:S(2)}) collective-permute-start(bf16[4,256,256]{2,1,0:T(8,128)(2,1)S(1)} %collective-permute-done.got), channel_id=1, source_target_pairs={{0,1},{1,0},{2,3},{3,2},{4,5},{5,4},{6,7},{7,6},{8,9},{9,8},{10,11... | collective-permute-start | bytes 1572872 | tf_op jit(solution)/shard_map/ppermute | solution.py:18
  37.6 10.8 %collective-permute-start.2 = (bf16[3,256,256]{2,1,0:T(8,128)(2,1)S(1)}, bf16[3,256,256]{2,1,0:T(8,128)(2,1)S(1)}, u32[]{:S(2)}, u32[]{:S(2)}) collective-permute-start(bf16[3,256,256]{2,1,0:T(8,128)(2,1)S(1)} %get-tuple-element.76), channel_id=1, source_target_pairs={{0,16},{16,0},{1,17},{17,1},{2,18},{18,2},{3,19},{19,3},{4,20},{20... | collective-permute-start | bytes 1179656 | tf_op jit(solution)/shard_map/ppermute | solution.py:18
  64.1 8.8 %collective-permute-start.12 = (bf16[2,2,256,128]{3,2,1,0:T(8,128)(2,1)S(1)}, bf16[2,2,256,128]{3,2,1,0:T(8,128)(2,1)S(1)}, u32[]{:S(2)}, u32[]{:S(2)}) collective-permute-start(bf16[2,2,256,128]{3,2,1,0:T(8,128)(2,1)S(1)} %add_convert_fusion.2.refs_0_), channel_id=1, source_target_pairs={{0,32},{32,64},{64,96},{96,128},{128,160},{160,192},{192,224},{224... | collective-permute-start | bytes 786440 | tf_op jit(solution)/shard_map/ppermute | solution.py:18
  81.5 9.2 %collective-permute-start.14 = (bf16[2,2,256,128]{3,2,1,0:T(8,128)(2,1)S(1)}, bf16[2,2,256,128]{3,2,1,0:T(8,128)(2,1)S(1)}, u32[]{:S(2)}, u32[]{:S(2)}) collective-permute-start(bf16[2,2,256,128]{3,2,1,0:T(8,128)(2,1)S(1)} %collective-permute-done.13.refs_5_), channel_id=1, source_target_pairs={{0,32},{32,64},{64,96},{96,128},{128,160},{160,192},{192,224},{224... | collective-permute-start | bytes 786440 | tf_op jit(solution)/shard_map/ppermute | solution.py:18
  81.5 9.2 %collective-permute-start.17 = (bf16[2,2,256,128]{3,2,1,0:T(8,128)(2,1)S(1)}, bf16[2,2,256,128]{3,2,1,0:T(8,128)(2,1)S(1)}, u32[]{:S(2)}, u32[]{:S(2)}) collective-permute-start(bf16[2,2,256,128]{3,2,1,0:T(8,128)(2,1)S(1)} %collective-permute-done.16.refs_2_), channel_id=1, source_target_pairs={{0,224},{32,0},{64,32},{96,64},{128,96},{160,128},{192,160},{224,1... | collective-permute-start | bytes 786440 | tf_op jit(solution)/shard_map/ppermute | solution.py:18
  84.2 20.9 %collective-permute-start.21 = (bf16[2048,256]{1,0:T(8,128)(2,1)}, bf16[2048,256]{1,0:T(8,128)(2,1)S(1)}, u32[]{:S(2)}, u32[]{:S(2)}) collective-permute-start(bf16[2048,256]{1,0:T(8,128)(2,1)} %all-gather.2.cloned.1.call-done.weight), channel_id=1, source_target_pairs={{0,16},{16,0},{1,17},{17,1},{2,18},{18,2},{3,19},{19,3},{4,20},{20... | collective-permute-start | bytes 3145736 | tf_op jit(solution)/shard_map/ppermute | solution.py:18
  90.6 14.5 %collective-permute-start.20 = (bf16[6,256,256]{2,1,0:T(8,128)(2,1)S(1)}, bf16[6,256,256]{2,1,0:T(8,128)(2,1)}, u32[]{:S(2)}, u32[]{:S(2)}) collective-permute-start(bf16[6,256,256]{2,1,0:T(8,128)(2,1)S(1)} %bitcast.13), channel_id=1, source_target_pairs={{0,224},{32,0},{64,32},{96,64},{128,96},{160,128},{192,160},{224,1... | collective-permute-start | bytes 2359304 | tf_op jit(solution)/shard_map/ppermute | solution.py:18
  98.9 14.9 %collective-permute-start.22 = (bf16[6,256,256]{2,1,0:T(8,128)(2,1)S(1)}, bf16[6,256,256]{2,1,0:T(8,128)(2,1)S(1)}, u32[]{:S(2)}, u32[]{:S(2)}) collective-permute-start(bf16[6,256,256]{2,1,0:T(8,128)(2,1)S(1)} %bitcast.14), channel_id=1, source_target_pairs={{0,32},{32,64},{64,96},{96,128},{128,160},{160,192},{192,224},{224... | collective-permute-start | bytes 2359304 | tf_op jit(solution)/shard_map/ppermute | solution.py:18
  113.8 14.0 %collective-permute-start.23 = (bf16[8,256,256]{2,1,0:T(8,128)(2,1)S(1)}, bf16[8,256,256]{2,1,0:T(8,128)(2,1)S(1)}, u32[]{:S(2)}, u32[]{:S(2)}) collective-permute-start(bf16[8,256,256]{2,1,0:T(8,128)(2,1)S(1)} %get-tuple-element.65), channel_id=1, source_target_pairs={{0,1},{1,0},{2,3},{3,2},{4,5},{5,4},{6,7},{7,6},{8,9},{9,8},{10,11... | collective-permute-start | bytes 3145736 | tf_op jit(solution)/shard_map/ppermute | solution.py:18
  125.5 19.5 %collective-permute-start.24 = (bf16[6,256,256]{2,1,0:T(8,128)(2,1)}, bf16[6,256,256]{2,1,0:T(8,128)(2,1)}, u32[]{:S(2)}, u32[]{:S(2)}) collective-permute-start(bf16[6,256,256]{2,1,0:T(8,128)(2,1)} %collective-permute-done.20.refs_1_), channel_id=1, source_target_pairs={{0,224},{32,0},{64,32},{96,64},{128,96},{160,128},{192,160},{224,1... | collective-permute-start | bytes 2359304 | tf_op jit(solution)/shard_map/ppermute | solution.py:18
  129.1 21.7 %all-to-all-start = ((bf16[8,256,256]{2,1,0:T(8,128)(2,1)}), bf16[8,256,256]{2,1,0:T(8,128)(2,1)}, u32[]{:S(2)}, u32[]{:S(2)}) async-start(bf16[8,256,256]{2,1,0:T(8,128)(2,1)} %add_convert_fusion.1), calls=%async_computation | async-start | bytes 2097152 | tf_op jit(solution)/shard_map/all_to_all | solution.py:268
  136.1 24.1 %collective-permute-start.27 = (bf16[6,256,256]{2,1,0:T(8,128)(2,1)}, bf16[6,256,256]{2,1,0:T(8,128)(2,1)}, u32[]{:S(2)}, u32[]{:S(2)}) collective-permute-start(bf16[6,256,256]{2,1,0:T(8,128)(2,1)} %copy-done.2), channel_id=1, source_target_pairs={{0,32},{32,64},{64,96},{96,128},{128,160},{160,192},{192,224},{224... | collective-permute-start | bytes 2359304 | tf_op jit(solution)/shard_map/ppermute | solution.py:18
  145.0 18.6 %collective-permute-start.25 = (bf16[6,256,256]{2,1,0:T(8,128)(2,1)}, bf16[6,256,256]{2,1,0:T(8,128)(2,1)}, u32[]{:S(2)}, u32[]{:S(2)}) collective-permute-start(bf16[6,256,256]{2,1,0:T(8,128)(2,1)} %collective-permute-done.24.refs_2_), channel_id=1, source_target_pairs={{0,224},{32,0},{64,32},{96,64},{128,96},{160,128},{192,160},{224,1... | collective-permute-start | bytes 2359304 | tf_op jit(solution)/shard_map/ppermute | solution.py:18
  154.7 27.1 %all-to-all-start.1 = ((bf16[8,256,256]{2,1,0:T(8,128)(2,1)}), bf16[8,256,256]{2,1,0:T(8,128)(2,1)}, u32[]{:S(2)}, u32[]{:S(2)}) async-start(bf16[8,256,256]{2,1,0:T(8,128)(2,1)} %copy-done.5), calls=%async_computation.1 | async-start | bytes 2097152 | tf_op jit(solution)/shard_map/all_to_all | solution.py:268
  160.3 19.8 %collective-permute-start.28 = (bf16[6,256,256]{2,1,0:T(8,128)(2,1)}, bf16[6,256,256]{2,1,0:T(8,128)(2,1)S(1)}, u32[]{:S(2)}, u32[]{:S(2)}) collective-permute-start(bf16[6,256,256]{2,1,0:T(8,128)(2,1)} %collective-permute-done.27.refs_6_), channel_id=1, source_target_pairs={{0,32},{32,64},{64,96},{96,128},{128,160},{160,192},{192,224},{224... | collective-permute-start | bytes 2359304 | tf_op jit(solution)/shard_map/ppermute | solution.py:18
  163.6 18.2 %collective-permute-start.26 = (bf16[6,256,256]{2,1,0:T(8,128)(2,1)}, bf16[6,256,256]{2,1,0:T(8,128)(2,1)S(1)}, u32[]{:S(2)}, u32[]{:S(2)}) collective-permute-start(bf16[6,256,256]{2,1,0:T(8,128)(2,1)} %collective-permute-done.25.refs_3_), channel_id=1, source_target_pairs={{0,224},{32,0},{64,32},{96,64},{128,96},{160,128},{192,160},{224,1... | collective-permute-start | bytes 2359304 | tf_op jit(solution)/shard_map/ppermute | solution.py:18
  (40 other events, 449.2 us)
Sparse Core Ops, SparseCore 0:
  39.0 33.1 all-gather.1

commit v3 on v2

--- a/solution.py
+++ b/solution.py
@@ -180,7 +180,10 @@
 def glu_kernel(where, mine, other, gain, *refs):
     pieces, (gated, normed, weights, sems) = refs[:-4], refs[-4:]
     blocks, rows, block = mine.shape
-    copies = fetch([piece.at[:4] for piece in pieces], [weights.at[j] for j in range(blocks)], sems)
+    sources = [piece.at[:4] for piece in pieces]
+    sources[4:6] = [pieces[4], pieces[5].at[:1]]
+    places = [weights.at[j] for j in range(4)] + [weights.at[4, :3], weights.at[4, 3:]] + [weights.at[j] for j in range(5, 8)]
+    copies = fetch(sources, places, sems)
     z, xl = where[0], where[1]
     same = where[2] == xl
     step_rows = 32
@@ -216,7 +219,9 @@
 
 def conv_kernel(where, gated, before, after, taps, scale, offset, *refs):
     pieces, (mine, other, padded, activated, weights, sems) = refs[:-6], refs[-6:]
-    copies = fetch([piece.at[4:] for piece in pieces], [weights.at[j] for j in range(len(pieces))], sems)
+    sources = [piece.at[4:] for n, piece in enumerate(pieces) if n not in (4, 5)]
+    sources.append(pieces[5].at[1:])
+    copies = fetch(sources, [weights.at[j] for j in (0, 1, 2, 3, 5, 6, 7, 4)], sems)
     rows = gated.shape[0]
     rim = before.shape[0]
     seq = where[0] * 2 + where[1]
@@ -346,14 +351,14 @@
         [S((rows, block), BF16), S((blocks, rows, block), BF16)],
         [pltpu.VMEM((rows, block), BF16), pltpu.SemaphoreType.DMA, pltpu.SemaphoreType.DMA((blocks,))], 16,
         10 * rows * block, 20 * rows * block, pinned=[frames], out_specs=[vmem(), hbm()])
-    late_l4 = shift(late_l3, "z", -1)
-    mine, late_l4, late_r3 = step((exchange(copies), late_l4, late_r3))
+    late_far = both_ways(late_r3[:3], late_l3[3:])
+    mine, *late_far = step((exchange(copies), *late_far))
     other = shift(mine, "c", 1)
-    late = [late, late_l1, late_l2, late_l3, late_l4, late_r3, late_r2, late_r1]
+    late = [late, late_l1, late_l2, late_l3, *late_far, late_r3, late_r2, late_r1]
     gated = run_kernel(
         glu_kernel, where, [mine, other, conv_norm_gain.reshape(1, width)],
         S((rows, block), BF16),
-        [pltpu.VMEM((2 * blocks, rows, block), BF16), pltpu.VMEM((blocks, 4, block, block), BF16), pltpu.SemaphoreType.DMA((blocks,))], 48,
+        [pltpu.VMEM((2 * blocks, rows, block), BF16), pltpu.VMEM((blocks, 4, block, block), BF16), pltpu.SemaphoreType.DMA((9,))], 48,
         4 * rows * block * width, 6 << 20, pinned=late)
     rim = 16
     before = shift(gated[rows - rim :], SEQ, 1)

time: 235 us -> 233 us (level)
  waiting for transfers between devices: 89.4 us -> 82.7 us
    ppermute x33 -> x34, waiting for transfers between devices: 85.1 us -> 78.9 us  [shift(): lax.ppermute(value, axis, [(i, (i + step) % count) for i in range(count)])]
    ppermute x33 -> x34, starting transfers between devices: 61.2 us -> 63.3 us  [shift(): lax.ppermute(value, axis, [(i, (i + step) % count) for i in range(count)])]
    unnamed x56 -> x52, local copies, waits for them, and re-layouts: 6 us -> 5.98 us
  transfers between devices with their start and end apart: 36 -> 37, of which waited for: 21 -> 22; matrix products, arithmetic and copies ran while one was open for 1% -> 2% of each run, Pallas kernels for 8% -> 8%
where the time goes in v3:
time: 233 us; the launch traced here: 232 us
  waiting for transfers between devices  82.7 us (35%)
  starting transfers between devices  75.6 us (32%)
  Pallas kernels  27.5 us (12%)
  blocking collectives  22 us (9%)
  between operations  13.7 us (6%)
  local copies, waits for them, and re-layouts  8.21 us (4%)
  other arithmetic  2.57 us (1%)
    ppermute x34, waiting for transfers between devices, shift(): lax.ppermute(value, axis, [(i, (i + step) % count) for i in range(count)])  78.9 us
    ppermute x34, starting transfers between devices, shift(): lax.ppermute(value, axis, [(i, (i + step) % count) for i in range(count)])  63.3 us
    pallas_call x8, Pallas kernels, run_kernel(): pl.pallas_call(body, out_shape=outs, in_specs=[smem()] + [vmem()] * len(a...  27.5 us
    all_to_all x1, blocking collectives, exchange(): return lax.all_to_all(parts, CHIPS, 0, 0, tiled=True)  22 us
    all_to_all x2, starting transfers between devices, exchange(): return lax.all_to_all(parts, CHIPS, 0, 0, tiled=True)  12.3 us
    unnamed x52, local copies, waits for them, and re-layouts  5.98 us
  transfers between devices with their start and end apart: 37, of which 22 were waited for; matrix products, arithmetic and copies ran while one was open for 2% of the time, Pallas kernels for 8%

profile of v3, /device:TPU:1, one launch (start us, length us, event | category | flops | bytes accessed | tf_op | source)
XLA Modules:
  0.0 232.3 jit_solution(4980527861133635096)
XLA Ops:
  6.5 6.4 %collective-permute-start.3 = (bf16[3,256,256]{2,1,0:T(8,128)(2,1)}, bf16[3,256,256]{2,1,0:T(8,128)(2,1)S(1)}, u32[]{:S(2)}, u32[]{:S(2)}) collective-permute-start(bf16[3,256,256]{2,1,0:T(8,128)(2,1)} %refs_0_.1), channel_id=1, source_target_pairs={{0,224},{32,0},{64,32},{96,64},{128,96},{160,128},{192,160},{224,1... | collective-permute-start | bytes 1179656 | tf_op jit(solution)/shard_map/ppermute | solution.py:18
  21.0 3.3 %collective-permute-start.4 = (bf16[3,256,256]{2,1,0:T(8,128)(2,1)S(1)}, bf16[3,256,256]{2,1,0:T(8,128)(2,1)}, u32[]{:S(2)}, u32[]{:S(2)}) collective-permute-start(bf16[3,256,256]{2,1,0:T(8,128)(2,1)S(1)} %collective-permute-done.3.refs_1_), channel_id=1, source_target_pairs={{0,224},{32,0},{64,32},{96,64},{128,96},{160,128},{192,160},{224,1... | collective-permute-start | bytes 1179656 | tf_op jit(solution)/shard_map/ppermute | solution.py:18
  24.4 6.8 %collective-permute-done.4.refs_2_ = bf16[3,256,256]{2,1,0:T(8,128)(2,1)} collective-permute-done((bf16[3,256,256]{2,1,0:T(8,128)(2,1)S(1)}, bf16[3,256,256]{2,1,0:T(8,128)(2,1)}, u32[]{:S(2)}, u32[]{:S(2)}) %collective-permute-start.4) | collective-permute-done | bytes 393248 | tf_op jit(solution)/shard_map/ppermute | solution.py:18
  31.2 3.5 %collective-permute-start.5 = (bf16[3,256,256]{2,1,0:T(8,128)(2,1)}, bf16[3,256,256]{2,1,0:T(8,128)(2,1)S(1)}, u32[]{:S(2)}, u32[]{:S(2)}) collective-permute-start(bf16[3,256,256]{2,1,0:T(8,128)(2,1)} %collective-permute-done.4.refs_2_), channel_id=1, source_target_pairs={{0,224},{32,0},{64,32},{96,64},{128,96},{160,128},{192,160},{224,1... | collective-permute-start | bytes 1179656 | tf_op jit(solution)/shard_map/ppermute | solution.py:18
  41.0 3.4 %collective-permute-start.10 = (bf16[3,128,256]{2,1,0:T(8,128)(2,1)S(1)}, bf16[3,128,256]{2,1,0:T(8,128)(2,1)S(1)}, u32[]{:S(2)}, u32[]{:S(2)}) collective-permute-start(bf16[3,128,256]{2,1,0:T(8,128)(2,1)S(1)} %slice.29), channel_id=1, source_target_pairs={{0,224},{32,0},{64,32},{96,64},{128,96},{160,128},{192,160},{224,1... | collective-permute-start | bytes 589832 | tf_op jit(solution)/shard_map/ppermute | solution.py:18
  44.5 3.9 %collective-permute-done.2 = bf16[3,256,256]{2,1,0:T(8,128)(2,1)S(1)} collective-permute-done((bf16[3,256,256]{2,1,0:T(8,128)(2,1)S(1)}, bf16[3,256,256]{2,1,0:T(8,128)(2,1)S(1)}, u32[]{:S(2)}, u32[]{:S(2)}) %collective-permute-start.2) | collective-permute-done | bytes 393248 | tf_op jit(solution)/shard_map/ppermute | solution.py:18
  50.9 6.1 %shard_map.101 = (f32[2,2,256,128]{3,2,1,0:T(8,128)}, f32[1,2,256,128]{3,2,1,0:T(8,128)}, bf16[3,2,256,128]{3,2,1,0:T(8,128)(2,1)}) custom-call(s32[5]{0:T(128)} %copy-done.6, bf16[8,256,256]{2,1,0:T(8,128)(2,1)} %copy-done.12, bf16[4,256,256]{2,1,0:T(8,128)(2,1)} %copy-done.20, bf16[4,256,256]{2,1,0:T(8,128)(2,1)} %copy-done.21, ...), custom_call_target="tpu_custom_call" | custom-call | flops 1610612736 | bytes 7340032 | tf_op jit(solution)/shard_map/pallas_call | solution.py:34
  58.4 5.9 %collective-permute-done.11.got = bf16[3,2,256,128]{3,2,1,0:T(8,128)(2,1)S(1)} collective-permute-done((bf16[3,2,256,128]{3,2,1,0:T(8,128)(2,1)}, bf16[3,2,256,128]{3,2,1,0:T(8,128)(2,1)S(1)}, u32[]{:S(2)}, u32[]{:S(2)}) %collective-permute-start.11) | collective-permute-done | bytes 393248 | tf_op jit(solution)/shard_map/ppermute | solution.py:18
  67.2 5.9 %collective-permute-done.12.refs_6_ = bf16[2,2,256,128]{3,2,1,0:T(8,128)(2,1)S(1)} collective-permute-done((bf16[2,2,256,128]{3,2,1,0:T(8,128)(2,1)S(1)}, bf16[2,2,256,128]{3,2,1,0:T(8,128)(2,1)S(1)}, u32[]{:S(2)}, u32[]{:S(2)}) %collective-permute-start.12) | collective-permute-done | bytes 262176 | tf_op jit(solution)/shard_map/ppermute | solution.py:18
  75.7 6.4 %collective-permute-done.13.refs_5_ = bf16[2,2,256,128]{3,2,1,0:T(8,128)(2,1)S(1)} collective-permute-done((bf16[2,2,256,128]{3,2,1,0:T(8,128)(2,1)S(1)}, bf16[2,2,256,128]{3,2,1,0:T(8,128)(2,1)S(1)}, u32[]{:S(2)}, u32[]{:S(2)}) %collective-permute-start.13) | collective-permute-done | bytes 262176 | tf_op jit(solution)/shard_map/ppermute | solution.py:18
  82.1 3.0 %collective-permute-start.17 = (bf16[2,2,256,128]{3,2,1,0:T(8,128)(2,1)S(1)}, bf16[2,2,256,128]{3,2,1,0:T(8,128)(2,1)S(1)}, u32[]{:S(2)}, u32[]{:S(2)}) collective-permute-start(bf16[2,2,256,128]{3,2,1,0:T(8,128)(2,1)S(1)} %collective-permute-done.16.refs_2_), channel_id=1, source_target_pairs={{0,224},{32,0},{64,32},{96,64},{128,96},{160,128},{192,160},{224,1... | collective-permute-start | bytes 786440 | tf_op jit(solution)/shard_map/ppermute | solution.py:18
  86.3 4.5 %collective-permute-done.14.refs_4_ = bf16[2,2,256,128]{3,2,1,0:T(8,128)(2,1)S(1)} collective-permute-done((bf16[2,2,256,128]{3,2,1,0:T(8,128)(2,1)S(1)}, bf16[2,2,256,128]{3,2,1,0:T(8,128)(2,1)S(1)}, u32[]{:S(2)}, u32[]{:S(2)}) %collective-permute-start.14) | collective-permute-done | bytes 262176 | tf_op jit(solution)/shard_map/ppermute | solution.py:18
  93.8 4.2 %shard_map.102 = (f32[2,256,128]{2,1,0:T(8,128)S(1)}, f32[2,256,128]{2,1,0:T(8,128)S(1)}, f32[2,256,128]{2,1,0:T(8,128)S(1)}) custom-call(s32[5]{0:T(128)S(1)} %copy-done.7, f32[1,2,256,128]{3,2,1,0:T(8,128)S(1)} %copy-done.4, bf16[3,2,256,128]{3,2,1,0:T(8,128)(2,1)S(1)} %collective-permute-done.11.got, ...), custom_call_target="tpu_custom_call" | custom-call | flops 939524096 | bytes 4194304 | tf_op jit(solution)/shard_map/pallas_call | solution.py:34
  106.8 7.3 %collective-permute-done.22.refs_8_ = bf16[6,256,256]{2,1,0:T(8,128)(2,1)} collective-permute-done((bf16[6,256,256]{2,1,0:T(8,128)(2,1)S(1)}, bf16[6,256,256]{2,1,0:T(8,128)(2,1)}, u32[]{:S(2)}, u32[]{:S(2)}) %collective-permute-start.22) | collective-permute-done | bytes 786464 | tf_op jit(solution)/shard_map/ppermute | solution.py:18
  114.1 12.2 %collective-permute-start.23 = (bf16[8,256,256]{2,1,0:T(8,128)(2,1)S(1)}, bf16[8,256,256]{2,1,0:T(8,128)(2,1)S(1)}, u32[]{:S(2)}, u32[]{:S(2)}) collective-permute-start(bf16[8,256,256]{2,1,0:T(8,128)(2,1)S(1)} %get-tuple-element.65), channel_id=1, source_target_pairs={{0,1},{1,0},{2,3},{3,2},{4,5},{5,4},{6,7},{7,6},{8,9},{9,8},{10,11... | collective-permute-start | bytes 3145736 | tf_op jit(solution)/shard_map/ppermute | solution.py:18
  129.9 6.5 %all-to-all-start = ((bf16[8,256,256]{2,1,0:T(8,128)(2,1)}), bf16[8,256,256]{2,1,0:T(8,128)(2,1)}, u32[]{:S(2)}, u32[]{:S(2)}) async-start(bf16[8,256,256]{2,1,0:T(8,128)(2,1)} %add_convert_fusion.1), calls=%async_computation | async-start | bytes 2097152 | tf_op jit(solution)/shard_map/all_to_all | solution.py:273
  136.4 9.4 %collective-permute-done.27.refs_2_ = bf16[6,256,256]{2,1,0:T(8,128)(2,1)} collective-permute-done((bf16[6,256,256]{2,1,0:T(8,128)(2,1)}, bf16[6,256,256]{2,1,0:T(8,128)(2,1)}, u32[]{:S(2)}, u32[]{:S(2)}) %collective-permute-start.27) | collective-permute-done | bytes 786464 | tf_op jit(solution)/shard_map/ppermute | solution.py:18
  147.3 3.8 %all-to-all-done.parts = bf16[8,256,256]{2,1,0:T(8,128)(2,1)} async-done(((bf16[8,256,256]{2,1,0:T(8,128)(2,1)}), bf16[8,256,256]{2,1,0:T(8,128)(2,1)}, u32[]{:S(2)}, u32[]{:S(2)}) %all-to-all-start) | async-done | bytes 1048608 | tf_op jit(solution)/shard_map/all_to_all | solution.py:273
  155.0 5.7 %all-to-all-start.1 = ((bf16[8,256,256]{2,1,0:T(8,128)(2,1)}), bf16[8,256,256]{2,1,0:T(8,128)(2,1)S(1)}, u32[]{:S(2)}, u32[]{:S(2)}) async-start(bf16[8,256,256]{2,1,0:T(8,128)(2,1)} %copy-done.3), calls=%async_computation.1 | async-start | bytes 2097152 | tf_op jit(solution)/shard_map/all_to_all | solution.py:273
  160.7 3.7 %collective-permute-done.28.refs_3_ = bf16[6,256,256]{2,1,0:T(8,128)(2,1)} collective-permute-done((bf16[6,256,256]{2,1,0:T(8,128)(2,1)}, bf16[6,256,256]{2,1,0:T(8,128)(2,1)}, u32[]{:S(2)}, u32[]{:S(2)}) %collective-permute-start.28) | collective-permute-done | bytes 786464 | tf_op jit(solution)/shard_map/ppermute | solution.py:18
  169.3 5.6 %collective-permute-done.29.refs_5_ = bf16[3,256,256]{2,1,0:T(8,128)(2,1)S(1)} collective-permute-done((bf16[3,256,256]{2,1,0:T(8,128)(2,1)S(1)}, bf16[3,256,256]{2,1,0:T(8,128)(2,1)S(1)}, u32[]{:S(2)}, u32[]{:S(2)}) %collective-permute-start.29) | collective-permute-done | bytes 393248 | tf_op jit(solution)/shard_map/ppermute | solution.py:18
  174.9 4.2 %collective-permute-done.26.refs_4_ = bf16[3,256,256]{2,1,0:T(8,128)(2,1)S(1)} collective-permute-done((bf16[3,256,256]{2,1,0:T(8,128)(2,1)S(1)}, bf16[3,256,256]{2,1,0:T(8,128)(2,1)S(1)}, u32[]{:S(2)}, u32[]{:S(2)}) %collective-permute-start.26) | collective-permute-done | bytes 393248 | tf_op jit(solution)/shard_map/ppermute | solution.py:18
  185.3 5.6 %shard_map.106.gated = bf16[256,256]{1,0:T(8,128)(2,1)S(1)} custom-call(s32[5]{0:T(128)S(1)} %copy-done.7, bf16[8,256,256]{2,1,0:T(8,128)(2,1)} %copy-done.13, bf16[8,256,256]{2,1,0:T(8,128)(2,1)} %copy-done.14, f32[1,4096]{1,0:T(1,128)S(1)} %bitcast.18, bf16[6,256,256]{2,1,0:T(8,128)(2,1)S(1)} %bitcast.15, ...), custom_call_target="tpu_custom_call" | custom-call | flops 1073741824 | bytes 6291456 | tf_op jit(solution)/shard_map/pallas_call | solution.py:34
  202.6 22.0 %all_to_all.15 = bf16[8,256,256]{2,1,0:T(8,128)(2,1)S(1)} all-to-all(bf16[8,256,256]{2,1,0:T(8,128)(2,1)S(1)} %add_convert_fusion), channel_id=1, replica_groups=mesh['z'=8,'xl'=2,'xh'=2,'y'=4,'c'=2] {'xh','y'}, dimensions={0} | all-to-all | bytes 2097152 | tf_op jit(solution)/shard_map/all_to_all | solution.py:273
  (127 shorter events, 69.1 us)
Async XLA Ops:
  6.5 78.6 %all-gather.2.cloned.1.call-start = ((), (), s32[]{:S(2)}) async-start(), calls=%async_computation.3 | async-start | bytes 1179648 | tf_op jit(solution)/shard_map/all_gather | solution.py:296
  6.5 14.5 %collective-permute-start.3 = (bf16[3,256,256]{2,1,0:T(8,128)(2,1)}, bf16[3,256,256]{2,1,0:T(8,128)(2,1)S(1)}, u32[]{:S(2)}, u32[]{:S(2)}) collective-permute-start(bf16[3,256,256]{2,1,0:T(8,128)(2,1)} %refs_0_.1), channel_id=1, source_target_pairs={{0,224},{32,0},{64,32},{96,64},{128,96},{160,128},{192,160},{224,1... | collective-permute-start | bytes 1179656 | tf_op jit(solution)/shard_map/ppermute | solution.py:18
  12.9 11.4 %collective-permute-start.6 = (bf16[3,256,256]{2,1,0:T(8,128)(2,1)}, bf16[3,256,256]{2,1,0:T(8,128)(2,1)S(1)}, u32[]{:S(2)}, u32[]{:S(2)}) collective-permute-start(bf16[3,256,256]{2,1,0:T(8,128)(2,1)} %refs_0_.1), channel_id=1, source_target_pairs={{0,32},{32,64},{64,96},{96,128},{128,160},{160,192},{192,224},{224... | collective-permute-start | bytes 1179656 | tf_op jit(solution)/shard_map/ppermute | solution.py:18
  19.2 15.5 %collective-permute-start = (bf16[4,256,256]{2,1,0:T(8,128)(2,1)S(1)}, bf16[4,256,256]{2,1,0:T(8,128)(2,1)S(1)}, u32[]{:S(2)}, u32[]{:S(2)}) collective-permute-start(bf16[4,256,256]{2,1,0:T(8,128)(2,1)S(1)} %get-tuple-element.41), channel_id=1, source_target_pairs={{0,16},{16,0},{1,17},{17,1},{2,18},{18,2},{3,19},{19,3},{4,20},{20... | collective-permute-start | bytes 1572872 | tf_op jit(solution)/shard_map/ppermute | solution.py:18
  21.0 10.2 %collective-permute-start.4 = (bf16[3,256,256]{2,1,0:T(8,128)(2,1)S(1)}, bf16[3,256,256]{2,1,0:T(8,128)(2,1)}, u32[]{:S(2)}, u32[]{:S(2)}) collective-permute-start(bf16[3,256,256]{2,1,0:T(8,128)(2,1)S(1)} %collective-permute-done.3.refs_1_), channel_id=1, source_target_pairs={{0,224},{32,0},{64,32},{96,64},{128,96},{160,128},{192,160},{224,1... | collective-permute-start | bytes 1179656 | tf_op jit(solution)/shard_map/ppermute | solution.py:18
  24.4 10.4 %collective-permute-start.7 = (bf16[3,256,256]{2,1,0:T(8,128)(2,1)S(1)}, bf16[3,256,256]{2,1,0:T(8,128)(2,1)}, u32[]{:S(2)}, u32[]{:S(2)}) collective-permute-start(bf16[3,256,256]{2,1,0:T(8,128)(2,1)S(1)} %collective-permute-done.6.refs_8_), channel_id=1, source_target_pairs={{0,32},{32,64},{64,96},{96,128},{128,160},{160,192},{192,224},{224... | collective-permute-start | bytes 1179656 | tf_op jit(solution)/shard_map/ppermute | solution.py:18
  31.2 9.8 %collective-permute-start.5 = (bf16[3,256,256]{2,1,0:T(8,128)(2,1)}, bf16[3,256,256]{2,1,0:T(8,128)(2,1)S(1)}, u32[]{:S(2)}, u32[]{:S(2)}) collective-permute-start(bf16[3,256,256]{2,1,0:T(8,128)(2,1)} %collective-permute-done.4.refs_2_), channel_id=1, source_target_pairs={{0,224},{32,0},{64,32},{96,64},{128,96},{160,128},{192,160},{224,1... | collective-permute-start | bytes 1179656 | tf_op jit(solution)/shard_map/ppermute | solution.py:18
  34.7 9.7 %collective-permute-start.8 = (bf16[3,256,256]{2,1,0:T(8,128)(2,1)}, bf16[3,256,256]{2,1,0:T(8,128)(2,1)S(1)}, u32[]{:S(2)}, u32[]{:S(2)}) collective-permute-start(bf16[3,256,256]{2,1,0:T(8,128)(2,1)} %collective-permute-done.7.refs_7_), channel_id=1, source_target_pairs={{0,32},{32,64},{64,96},{96,128},{128,160},{160,192},{192,224},{224... | collective-permute-start | bytes 1179656 | tf_op jit(solution)/shard_map/ppermute | solution.py:18
  34.8 13.7 %collective-permute-start.1 = (bf16[4,256,256]{2,1,0:T(8,128)(2,1)S(1)}, bf16[4,256,256]{2,1,0:T(8,128)(2,1)S(1)}, u32[]{:S(2)}, u32[]{:S(2)}) collective-permute-start(bf16[4,256,256]{2,1,0:T(8,128)(2,1)S(1)} %collective-permute-done.got), channel_id=1, source_target_pairs={{0,1},{1,0},{2,3},{3,2},{4,5},{5,4},{6,7},{7,6},{8,9},{9,8},{10,11... | collective-permute-start | bytes 1572872 | tf_op jit(solution)/shard_map/ppermute | solution.py:18
  37.7 10.8 %collective-permute-start.2 = (bf16[3,256,256]{2,1,0:T(8,128)(2,1)S(1)}, bf16[3,256,256]{2,1,0:T(8,128)(2,1)S(1)}, u32[]{:S(2)}, u32[]{:S(2)}) collective-permute-start(bf16[3,256,256]{2,1,0:T(8,128)(2,1)S(1)} %get-tuple-element.76), channel_id=1, source_target_pairs={{0,16},{16,0},{1,17},{17,1},{2,18},{18,2},{3,19},{19,3},{4,20},{20... | collective-permute-start | bytes 1179656 | tf_op jit(solution)/shard_map/ppermute | solution.py:18
  73.0 9.1 %collective-permute-start.13 = (bf16[2,2,256,128]{3,2,1,0:T(8,128)(2,1)S(1)}, bf16[2,2,256,128]{3,2,1,0:T(8,128)(2,1)S(1)}, u32[]{:S(2)}, u32[]{:S(2)}) collective-permute-start(bf16[2,2,256,128]{3,2,1,0:T(8,128)(2,1)S(1)} %collective-permute-done.12.refs_6_), channel_id=1, source_target_pairs={{0,32},{32,64},{64,96},{96,128},{128,160},{160,192},{192,224},{224... | collective-permute-start | bytes 786440 | tf_op jit(solution)/shard_map/ppermute | solution.py:18
  73.0 9.1 %collective-permute-start.16 = (bf16[2,2,256,128]{3,2,1,0:T(8,128)(2,1)S(1)}, bf16[2,2,256,128]{3,2,1,0:T(8,128)(2,1)S(1)}, u32[]{:S(2)}, u32[]{:S(2)}) collective-permute-start(bf16[2,2,256,128]{3,2,1,0:T(8,128)(2,1)S(1)} %collective-permute-done.15.refs_1_), channel_id=1, source_target_pairs={{0,224},{32,0},{64,32},{96,64},{128,96},{160,128},{192,160},{224,1... | collective-permute-start | bytes 786440 | tf_op jit(solution)/shard_map/ppermute | solution.py:18
  85.2 20.4 %collective-permute-start.21 = (bf16[2048,256]{1,0:T(8,128)(2,1)}, bf16[2048,256]{1,0:T(8,128)(2,1)S(1)}, u32[]{:S(2)}, u32[]{:S(2)}) collective-permute-start(bf16[2048,256]{1,0:T(8,128)(2,1)} %all-gather.2.cloned.1.call-done.weight), channel_id=1, source_target_pairs={{0,16},{16,0},{1,17},{17,1},{2,18},{18,2},{3,19},{19,3},{4,20},{20... | collective-permute-start | bytes 3145736 | tf_op jit(solution)/shard_map/ppermute | solution.py:18
  90.8 14.7 %collective-permute-start.20 = (bf16[6,256,256]{2,1,0:T(8,128)(2,1)S(1)}, bf16[6,256,256]{2,1,0:T(8,128)(2,1)}, u32[]{:S(2)}, u32[]{:S(2)}) collective-permute-start(bf16[6,256,256]{2,1,0:T(8,128)(2,1)S(1)} %bitcast.13), channel_id=1, source_target_pairs={{0,224},{32,0},{64,32},{96,64},{128,96},{160,128},{192,160},{224,1... | collective-permute-start | bytes 2359304 | tf_op jit(solution)/shard_map/ppermute | solution.py:18
  99.1 15.0 %collective-permute-start.22 = (bf16[6,256,256]{2,1,0:T(8,128)(2,1)S(1)}, bf16[6,256,256]{2,1,0:T(8,128)(2,1)}, u32[]{:S(2)}, u32[]{:S(2)}) collective-permute-start(bf16[6,256,256]{2,1,0:T(8,128)(2,1)S(1)} %bitcast.14), channel_id=1, source_target_pairs={{0,32},{32,64},{64,96},{96,128},{128,160},{160,192},{192,224},{224... | collective-permute-start | bytes 2359304 | tf_op jit(solution)/shard_map/ppermute | solution.py:18
  114.1 14.5 %collective-permute-start.23 = (bf16[8,256,256]{2,1,0:T(8,128)(2,1)S(1)}, bf16[8,256,256]{2,1,0:T(8,128)(2,1)S(1)}, u32[]{:S(2)}, u32[]{:S(2)}) collective-permute-start(bf16[8,256,256]{2,1,0:T(8,128)(2,1)S(1)} %get-tuple-element.65), channel_id=1, source_target_pairs={{0,1},{1,0},{2,3},{3,2},{4,5},{5,4},{6,7},{7,6},{8,9},{9,8},{10,11... | collective-permute-start | bytes 3145736 | tf_op jit(solution)/shard_map/ppermute | solution.py:18
  126.3 19.5 %collective-permute-start.27 = (bf16[6,256,256]{2,1,0:T(8,128)(2,1)}, bf16[6,256,256]{2,1,0:T(8,128)(2,1)}, u32[]{:S(2)}, u32[]{:S(2)}) collective-permute-start(bf16[6,256,256]{2,1,0:T(8,128)(2,1)} %collective-permute-done.20.refs_1_), channel_id=1, source_target_pairs={{0,224},{32,0},{64,32},{96,64},{128,96},{160,128},{192,160},{224,1... | collective-permute-start | bytes 2359304 | tf_op jit(solution)/shard_map/ppermute | solution.py:18
  126.6 20.7 %collective-permute-start.24 = (bf16[6,256,256]{2,1,0:T(8,128)(2,1)}, bf16[6,256,256]{2,1,0:T(8,128)(2,1)}, u32[]{:S(2)}, u32[]{:S(2)}) collective-permute-start(bf16[6,256,256]{2,1,0:T(8,128)(2,1)} %collective-permute-done.22.refs_8_), channel_id=1, source_target_pairs={{0,32},{32,64},{64,96},{96,128},{128,160},{160,192},{192,224},{224... | collective-permute-start | bytes 2359304 | tf_op jit(solution)/shard_map/ppermute | solution.py:18
  129.9 21.2 %all-to-all-start = ((bf16[8,256,256]{2,1,0:T(8,128)(2,1)}), bf16[8,256,256]{2,1,0:T(8,128)(2,1)}, u32[]{:S(2)}, u32[]{:S(2)}) async-start(bf16[8,256,256]{2,1,0:T(8,128)(2,1)} %add_convert_fusion.1), calls=%async_computation | async-start | bytes 2097152 | tf_op jit(solution)/shard_map/all_to_all | solution.py:273
  145.8 18.6 %collective-permute-start.28 = (bf16[6,256,256]{2,1,0:T(8,128)(2,1)}, bf16[6,256,256]{2,1,0:T(8,128)(2,1)}, u32[]{:S(2)}, u32[]{:S(2)}) collective-permute-start(bf16[6,256,256]{2,1,0:T(8,128)(2,1)} %collective-permute-done.27.refs_2_), channel_id=1, source_target_pairs={{0,224},{32,0},{64,32},{96,64},{128,96},{160,128},{192,160},{224,1... | collective-permute-start | bytes 2359304 | tf_op jit(solution)/shard_map/ppermute | solution.py:18
  147.3 20.9 %collective-permute-start.25 = (bf16[6,256,256]{2,1,0:T(8,128)(2,1)}, bf16[6,256,256]{2,1,0:T(8,128)(2,1)}, u32[]{:S(2)}, u32[]{:S(2)}) collective-permute-start(bf16[6,256,256]{2,1,0:T(8,128)(2,1)} %collective-permute-done.24.refs_7_), channel_id=1, source_target_pairs={{0,32},{32,64},{64,96},{96,128},{128,160},{160,192},{192,224},{224... | collective-permute-start | bytes 2359304 | tf_op jit(solution)/shard_map/ppermute | solution.py:18
  155.0 24.2 %all-to-all-start.1 = ((bf16[8,256,256]{2,1,0:T(8,128)(2,1)}), bf16[8,256,256]{2,1,0:T(8,128)(2,1)S(1)}, u32[]{:S(2)}, u32[]{:S(2)}) async-start(bf16[8,256,256]{2,1,0:T(8,128)(2,1)} %copy-done.3), calls=%async_computation.1 | async-start | bytes 2097152 | tf_op jit(solution)/shard_map/all_to_all | solution.py:273
  165.5 9.4 %collective-permute-start.29 = (bf16[3,256,256]{2,1,0:T(8,128)(2,1)S(1)}, bf16[3,256,256]{2,1,0:T(8,128)(2,1)S(1)}, u32[]{:S(2)}, u32[]{:S(2)}) collective-permute-start(bf16[3,256,256]{2,1,0:T(8,128)(2,1)S(1)} %slice.31), channel_id=1, source_target_pairs={{0,224},{32,0},{64,32},{96,64},{128,96},{160,128},{192,160},{224,1... | collective-permute-start | bytes 1179656 | tf_op jit(solution)/shard_map/ppermute | solution.py:18
  169.2 9.9 %collective-permute-start.26 = (bf16[3,256,256]{2,1,0:T(8,128)(2,1)S(1)}, bf16[3,256,256]{2,1,0:T(8,128)(2,1)S(1)}, u32[]{:S(2)}, u32[]{:S(2)}) collective-permute-start(bf16[3,256,256]{2,1,0:T(8,128)(2,1)S(1)} %slice.30), channel_id=1, source_target_pairs={{0,32},{32,64},{64,96},{96,128},{128,160},{160,192},{192,224},{224... | collective-permute-start | bytes 1179656 | tf_op jit(solution)/shard_map/ppermute | solution.py:18
  (39 other events, 422.3 us)
Sparse Core Ops, SparseCore 0:
  39.1 33.1 all-gather.1
